TPU v7x, 256 devices: a whole 4x4x8 slice. The times are simulated.
256 devices in a mesh: grp: 32 (over z, y), tp: 8 (over x, core).
Axes of the slice: x: 4, y: 4, z: 8, core: 2. Of those that a mesh axis runs over, the one named last changes fastest.
Arguments:
- queries: bfloat16 [512, 6144], P('grp', 'tp'), may hold values from -16 to 16
- new_keys: bfloat16 [512, 1024], P('grp', 'tp'), may hold values from -4 to 4
- new_values: bfloat16 [512, 1024], P('grp', 'tp'), may hold values from -4 to 4
- key_cache: bfloat16 [512, 256, 1024], P('grp', None, 'tp'), may hold values from -16 to 16
- value_cache: bfloat16 [512, 256, 1024], P('grp', None, 'tp'), may hold values from -4 to 4
- cache_lengths: int32 [512], P('grp'), may hold values from 2 to 256
- hidden_b: bfloat16 [512, 6144], P('grp', 'tp'), may hold values from -400 to 400
- norm_gain: float32 [6144], replicated, may hold values from 0.5 to 2
- routes: int32 [512, 2], P('grp'), may hold values from 0 to 3, all different within a row; in each aligned block of 16 rows (0 to 15, 16 to 31, ...) at most 12 rows name the same one
- route_gates: float32 [512, 2], P('grp'), may hold values from 0.5 to 1.5
- w_gate: bfloat16 [32, 6144, 2048], P('grp', None, 'tp'), may hold values from -0.078125 to 0.078125
- w_up: bfloat16 [32, 6144, 2048], P('grp', None, 'tp'), may hold values from -0.078125 to 0.078125
- w_down: bfloat16 [32, 2048, 6144], P('grp', 'tp'), may hold values from -0.046875 to 0.046875
Outputs:
- attention_a: bfloat16 [512, 6144], P('grp', 'tp')
- expert_b: bfloat16 [512, 6144], P('grp', 'tp')
Inputs may be any that keep to these rules, and one draw needn't show every extreme that they name: `routes`: each row names 2 different experts. In each aligned block of 16 rows (the rows of one index of grp) no expert is named by more than 12 rows.
All inputs are finite; a program needn't handle non-finite values.
Results may differ from a plain program's by a relative error of at most 0.0065.
Values may be sent and summed in bfloat16 or wider, within the bound.
No kernel may reach another device: no remote copies, remote signals or barrier semaphores. Data moves between devices by JAX's collectives and lax.ppermute only.
A program may use at most 128 MiB of HBM per device.

v0:
```python
import jax
import jax.numpy as jnp
from jax import lax
from jax.sharding import PartitionSpec as P

HEADS = 48
KV_HEADS = 8
HEAD_DIM = 128
EXPERTS = 4
TOP = 2


def attend(queries, new_keys, new_values, key_cache, value_cache, cache_lengths):
    row_count = queries.shape[0]
    slot_count = key_cache.shape[1]
    kv_local = new_keys.shape[1] // HEAD_DIM
    per_group = HEADS // KV_HEADS
    query_heads = queries.reshape(row_count, kv_local, per_group, HEAD_DIM)
    key_heads = key_cache.reshape(row_count, slot_count, kv_local, HEAD_DIM)
    value_heads = value_cache.reshape(row_count, slot_count, kv_local, HEAD_DIM)
    own_key = new_keys.reshape(row_count, kv_local, HEAD_DIM)
    own_value = new_values.reshape(row_count, kv_local, HEAD_DIM)
    inv_root = 1.0 / HEAD_DIM**0.5
    scores = (
        jnp.einsum("rkgd,rckd->rkgc", query_heads, key_heads, preferred_element_type=jnp.float32)
        * inv_root
    )
    own_score = (
        jnp.einsum("rkgd,rkd->rkg", query_heads, own_key, preferred_element_type=jnp.float32)
        * inv_root
    )
    visible = (jnp.arange(slot_count, dtype=jnp.int32)[None, :] < cache_lengths[:, None])[
        :, None, None, :
    ]
    scores = jnp.where(visible, scores, -1e30)
    peak_score = jnp.maximum(jnp.max(scores, axis=-1), own_score)
    weights = jnp.where(visible, jnp.exp(scores - peak_score[..., None]), 0.0)
    own_weight = jnp.exp(own_score - peak_score)
    denominator = jnp.sum(weights, axis=-1) + own_weight
    probabilities = (weights / denominator[..., None]).astype(jnp.bfloat16)
    own_prob = (own_weight / denominator).astype(jnp.bfloat16)
    mixed = jnp.einsum(
        "rkgc,rckd->rkgd", probabilities, value_heads, preferred_element_type=jnp.float32
    )
    mixed = (
        mixed
        + own_prob.astype(jnp.float32)[..., None] * own_value.astype(jnp.float32)[:, :, None, :]
    )
    return mixed.astype(jnp.bfloat16).reshape(row_count, kv_local * per_group * HEAD_DIM)


def route_tables(routes, route_gates, capacity):
    row_count = routes.shape[0]
    chosen = routes.reshape(row_count * TOP)
    onehot = (chosen[:, None] == jnp.arange(EXPERTS, dtype=jnp.int32)[None, :]).astype(jnp.int32)
    rank_run = jnp.cumsum(onehot, axis=0) - onehot
    slot_ids = jnp.sum(rank_run * onehot, axis=1)
    target = chosen * capacity + slot_ids
    matches = target[None, :] == jnp.arange(EXPERTS * capacity, dtype=jnp.int32)[:, None]
    placing = jnp.sum(
        matches.astype(jnp.float32).reshape(EXPERTS * capacity, row_count, TOP), axis=2
    ).astype(jnp.bfloat16)
    spread = matches.astype(jnp.float32).T.reshape(row_count, TOP, EXPERTS * capacity)
    weights = jnp.sum(spread * route_gates[:, :, None], axis=1)
    return (placing, weights)


def local(
    queries,
    new_keys,
    new_values,
    key_cache,
    value_cache,
    cache_lengths,
    hidden_b,
    norm_gain,
    routes,
    route_gates,
    w_gate,
    w_up,
    w_down,
):
    attention_a = attend(queries, new_keys, new_values, key_cache, value_cache, cache_lengths)
    groups = lax.axis_size("grp")
    row_count = hidden_b.shape[0]
    capacity = 3 * row_count // 4
    copies = groups // EXPERTS
    placing, weights = route_tables(routes, route_gates, capacity)
    gate_part = w_gate[0]
    up_part = w_up[0]
    down_part = w_down[0]
    full_rows = lax.all_gather(hidden_b, "tp", axis=1, tiled=True).astype(jnp.float32)
    inv_scale = lax.rsqrt(jnp.mean(full_rows * full_rows, axis=1, keepdims=True) + 1e-05)
    normed = (full_rows * inv_scale * norm_gain[None, :]).astype(jnp.bfloat16)
    packed = jnp.dot(placing, normed, preferred_element_type=jnp.float32).astype(jnp.bfloat16)
    row_width = packed.shape[1]
    outgoing = jnp.broadcast_to(
        packed.reshape(1, EXPERTS, capacity, row_width), (copies, EXPERTS, capacity, row_width)
    ).reshape(groups, capacity, row_width)
    incoming = lax.all_to_all(outgoing, "grp", split_axis=0, concat_axis=0, tiled=True).reshape(
        groups * capacity, row_width
    )
    gate_sum = jnp.dot(incoming, gate_part, preferred_element_type=jnp.float32)
    up_sum = jnp.dot(incoming, up_part, preferred_element_type=jnp.float32)
    activated = (jax.nn.silu(gate_sum) * up_sum).astype(jnp.bfloat16)
    partial_value = jnp.dot(activated, down_part, preferred_element_type=jnp.float32)
    shares = lax.psum_scatter(partial_value, "tp", scatter_dimension=1, tiled=True)
    returned = lax.all_to_all(
        shares.reshape(groups, capacity, shares.shape[1]),
        "grp",
        split_axis=0,
        concat_axis=0,
        tiled=True,
    )
    summed = jnp.sum(returned.reshape(copies, EXPERTS * capacity, returned.shape[2]), axis=0)
    expert_b = jnp.dot(
        weights, summed, precision=lax.Precision.HIGHEST, preferred_element_type=jnp.float32
    ).astype(jnp.bfloat16)
    return (attention_a, expert_b)


def solution(mesh):
    placed = (
        P("grp", "tp"),
        P("grp", "tp"),
        P("grp", "tp"),
        P("grp", None, "tp"),
        P("grp", None, "tp"),
        P("grp"),
        P("grp", "tp"),
        P(),
        P("grp", None),
        P("grp", None),
        P("grp", None, "tp"),
        P("grp", None, "tp"),
        P("grp", "tp", None),
    )
    return jax.shard_map(
        local,
        mesh=mesh,
        in_specs=placed,
        out_specs=(P("grp", "tp"), P("grp", "tp")),
        check_vma=False,
    )
```

profile of v0, /device:TPU:8, one launch (start us, length us, event | category | flops | bytes accessed | tf_op | source)
XLA Modules:
  0.0 325.1 jit_solution(10422812595427857208)
XLA Ops:
  7.2 0.0 copy-start
  7.2 0.0 reduce-scatter.2.cloned.1.call-start
  7.2 0.9 copy.28
  8.1 0.1 eq.37
  8.2 0.1 fusion.33
  8.3 0.1 reduce_window_sum.11
  8.4 0.2 select_reduce_fusion.1
  8.5 0.1 reduce_sum.58
  8.6 0.1 copy.29
  8.7 0.7 multiply_add_fusion
  9.4 0.1 convert_reduce_fusion
  9.5 13.4 %all_gather.3 = bf16[16,6144]{1,0:T(8,128)(2,1)S(1)} all-gather(bf16[16,768]{1,0:T(8,128)(2,1)} %param.19), channel_id=1, replica_groups=mesh['grp'=32,'tp'=8] {'tp'}, dimensions={1}, use_global_device_ids=true | all-gather | bytes 221184 | tf_op jit(solution)/shard_map/all_gather | solution.py:92
  22.8 0.2 fusion.16
  23.0 1.9 convolution_convert_fusion
  24.9 2.1 broadcast_in_dim.41
  27.0 1.9 broadcast_in_dim.42
  28.9 152.5 %all_to_all.10 = bf16[32,12,6144]{2,1,0:T(8,128)(2,1)} all-to-all(bf16[32,12,6144]{2,1,0:T(8,128)(2,1)S(1)} %bitcast.32), channel_id=1, replica_groups=mesh['grp'=32,'tp'=8] {'grp'}, dimensions={0} | all-to-all | bytes 9437184 | tf_op jit(solution)/shard_map/all_to_all | solution.py:100
  181.5 7.6 %reshape.145 = bf16[384,6144]{1,0:T(8,128)(2,1)} reshape(bf16[32,12,6144]{2,1,0:T(8,128)(2,1)} %all_to_all.10) | data formatting | bytes 9437184 | tf_op jit(solution)/shard_map/reshape | solution.py:100
  189.0 4.7 %fusion.4 = f32[384,256]{1,0:T(8,128)S(1)} fusion(bf16[384,6144]{1,0:T(8,128)(2,1)} %reshape.145, bf16[1,6144,256]{2,1,0:T(8,128)(2,1)} %param.23), kind=kOutput, calls=%fused_computation.5 | convolution fusion | flops 1207959552 | bytes 8257536 | tf_op jit(solution)/shard_map/dot_general | solution.py:103
  193.7 0.0 copy-done
  193.7 12.0 %fusion = f32[384,6144]{1,0:T(8,128)} fusion(bf16[1,256,6144]{2,1,0:T(8,128)(2,1)S(1)} %copy-done, bf16[384,6144]{1,0:T(8,128)(2,1)} %reshape.145, bf16[1,6144,256]{2,1,0:T(8,128)(2,1)} %param.24, f32[384,256]{1,0:T(8,128)S(1)} %fusion.4), kind=kOutput, calls=%fused_computation.1 | convolution fusion | flops 2416508928 | bytes 20840448 | tf_op jit(solution)/shard_map/dot_general | solution.py:106
  205.8 0.0 reduce-scatter.2.cloned.1.call-update
  205.8 0.0 copy-start.1
  205.8 0.0 copy-start.2
  205.8 0.0 copy-start.4
  205.8 0.0 copy-start.5
  205.8 56.2 %reduce-scatter.2.cloned.1.call-done = f32[384,768]{1,0:T(8,128)} async-done(((f32[384,6144]{1,0:T(8,128)}), f32[384,768]{1,0:T(8,128)}) %reduce-scatter.2.cloned.1.call-update) | async-done | bytes 1179664 | tf_op jit(solution)/shard_map/reduce_scatter | solution.py:107
  262.0 2.5 reshape.146
  264.4 0.0 copy-start.3
  264.5 10.3 %all-to-all-start.1 = ((f32[32,12,768]{2,1,0:T(8,128)}), f32[32,12,768]{2,1,0:T(8,128)}, u32[]{:S(2)}, u32[]{:S(2)}) async-start(f32[32,12,768]{2,1,0:T(8,128)} %reshape.146), calls=%async_computation.2 | async-start | bytes 3145728 | tf_op jit(solution)/shard_map/all_to_all | solution.py:108
  274.8 0.0 copy-done.1
  274.8 0.1 reshape.142
  274.9 0.0 copy-done.2
  274.9 0.0 copy-done.4
  274.9 0.1 iota_compare_fusion.3
  275.0 0.0 copy-done.5
  275.0 0.1 fusion.34
  275.1 1.7 fusion.41
  276.8 0.2 fusion.28
  277.0 1.5 fusion.15
  278.6 0.6 copy.36
  279.2 0.0 copy-done.3
  279.2 0.1 select_reduce_fusion
  279.3 34.4 %all-to-all-done.1 = f32[32,12,768]{2,1,0:T(8,128)} async-done(((f32[32,12,768]{2,1,0:T(8,128)}), f32[32,12,768]{2,1,0:T(8,128)}, u32[]{:S(2)}, u32[]{:S(2)}) %all-to-all-start.1) | async-done | bytes 1179680 | tf_op jit(solution)/shard_map/all_to_all | solution.py:108
  313.6 2.4 reshape.147
  316.1 1.3 reduce_sum.62
  317.4 0.8 convolution_convert_fusion.1
  (4 shorter events, 0.0 us)
Async XLA Ops:
  7.2 186.6 %copy-start = (bf16[1,256,6144]{2,1,0:T(8,128)(2,1)S(1)}, bf16[1,256,6144]{2,1,0:T(8,128)(2,1)}, u32[]{:S(2)}) copy-start(bf16[1,256,6144]{2,1,0:T(8,128)(2,1)} %param.25) | copy-start | bytes 9437188
  7.2 254.8 %reduce-scatter.2.cloned.1.call-start = ((), (), s32[]{:S(2)}) async-start(), calls=%async_computation.3 | async-start | bytes 10616832 | tf_op jit(solution)/shard_map/reduce_scatter | solution.py:107
  205.8 69.0 %copy-start.1 = (bf16[16,768]{1,0:T(8,128)(2,1)S(1)}, bf16[16,768]{1,0:T(8,128)(2,1)}, u32[]{:S(2)}) copy-start(bf16[16,768]{1,0:T(8,128)(2,1)} %param.13) | copy-start | bytes 73732
  205.8 69.1 %copy-start.2 = (bf16[16,128]{1,0:T(8,128)(2,1)S(1)}, bf16[16,128]{1,0:T(8,128)(2,1)}, u32[]{:S(2)}) copy-start(bf16[16,128]{1,0:T(8,128)(2,1)} %param.15) | copy-start | bytes 12292
  205.8 69.1 %copy-start.4 = (s32[16]{0:T(128)S(1)}, s32[16]{0:T(128)}, u32[]{:S(2)}) copy-start(s32[16]{0:T(128)} %param.18) | copy-start | bytes 196
  205.8 69.2 %copy-start.5 = (bf16[16,128]{1,0:T(8,128)(2,1)S(1)}, bf16[16,128]{1,0:T(8,128)(2,1)}, u32[]{:S(2)}) copy-start(bf16[16,128]{1,0:T(8,128)(2,1)} %param.14) | copy-start | bytes 12292
  264.4 14.7 %copy-start.3 = (f32[16,2]{0,1:T(2,128)S(1)}, f32[16,2]{0,1:T(2,128)}, u32[]{:S(2)}) copy-start(f32[16,2]{0,1:T(2,128)} %param.22) | copy-start | bytes 388
  264.5 49.2 %all-to-all-start.1 = ((f32[32,12,768]{2,1,0:T(8,128)}), f32[32,12,768]{2,1,0:T(8,128)}, u32[]{:S(2)}, u32[]{:S(2)}) async-start(f32[32,12,768]{2,1,0:T(8,128)} %reshape.146), calls=%async_computation.2 | async-start | bytes 3145728 | tf_op jit(solution)/shard_map/all_to_all | solution.py:108
Sparse Core Ops, SparseCore 0:
  205.9 56.0 reduce-scatter.1
where the time goes:
time: 326 us; the launch traced here: 325 us
  blocking collectives  166 us (51%)
  waiting for transfers between devices  90.5 us (28%)
  matrix products  22.8 us (7%)
  local copies, waits for them, and re-layouts  18.3 us (6%)
  between operations  14.2 us (4%)
  starting transfers between devices  10.4 us (3%)
    all_to_all x1, blocking collectives, local(): lax.all_to_all(outgoing, 'grp', split_axis=0, concat_axis=0, tiled=True)  153 us
    reduce_scatter x1, waiting for transfers between devices, local(): lax.psum_scatter(partial_value, 'tp', scatter_dimension=1, tiled=True)  56.2 us
    all_to_all x1, waiting for transfers between devices, local(): lax.all_to_all(shares.reshape(groups, capacity, shares.shape[1]), 'grp',...  34.4 us
    all_gather x1, blocking collectives, local(): lax.all_gather(hidden_b, 'tp', axis=1, tiled=True).astype(jnp.float32)  13.4 us
    dot_general x1, matrix products, local(): jnp.dot(activated, down_part, preferred_element_type=jnp.float32)  12 us
    all_to_all x1, starting transfers between devices, local(): lax.all_to_all(shares.reshape(groups, capacity, shares.shape[1]), 'grp',...  10.3 us
    reshape x1, local copies, waits for them, and re-layouts, local(): lax.all_to_all(outgoing, 'grp', split_axis=0, concat_axis=0, tiled=True)  7.57 us
  transfers between devices with their start and end apart: 2, of which 2 were waited for; matrix products, arithmetic and copies ran while one was open for 1% of the time, Pallas kernels for 0%

commit v1 on v0

v1 whole, which is shorter than its diff:
```python
import functools

import jax
import jax.numpy as jnp
from jax import lax
from jax.experimental import pallas as pl
from jax.experimental.pallas import tpu as pltpu
from jax.sharding import PartitionSpec as P

HEAD_DIM = 128
EXPERTS = 4
TOP = 2
NZ, NY, NX = 8, 4, 4
CAP = 12
NEAR = (0, 1, -1, 2, -2)
FAR = (3, 4, -3)
VMEM_LIMIT = 24 * 1024 * 1024
VMEM = pl.BlockSpec(memory_space=pltpu.VMEM)
ANY = pl.BlockSpec(memory_space=pl.ANY)
SMEM = pl.BlockSpec(memory_space=pltpu.SMEM)


def attend_kernel(lengths, queries, new_keys, new_values, key_cache, value_cache, out, q_buf, o_buf):
    f32, bf16 = jnp.float32, jnp.bfloat16
    count, slots, depth = key_cache.shape
    heads = queries.shape[1] // depth
    q_buf[...] = jnp.zeros_like(q_buf)
    for h in range(heads):
        q_buf[:, h, :] = queries[:, h * depth : (h + 1) * depth].astype(f32)
    own_keys = new_keys[...].astype(f32)
    own_values = new_values[...].astype(f32)
    inv_root = 1.0 / depth**0.5
    slot = lax.broadcasted_iota(jnp.int32, (q_buf.shape[1], slots), 1)
    for r in range(count):
        q = q_buf[r]
        scores = inv_root * lax.dot_general(
            q.astype(bf16), key_cache[r], (((1,), (1,)), ((), ())), preferred_element_type=f32
        )
        own = inv_root * jnp.sum(q * own_keys[r : r + 1], axis=1, keepdims=True)
        visible = slot < lengths[r]
        peak = jnp.max(jnp.where(visible, scores, -1e30), axis=1, keepdims=True)
        peak = jnp.maximum(peak, own)
        weights = jnp.where(visible, jnp.exp(scores - peak), 0.0)
        own_weight = jnp.exp(own - peak)
        total = jnp.sum(weights, axis=1, keepdims=True) + own_weight
        probs = (weights / total).astype(bf16)
        own_prob = (own_weight / total).astype(bf16).astype(f32)
        mixed = jnp.dot(probs, value_cache[r], preferred_element_type=f32)
        o_buf[r] = mixed + own_prob * own_values[r : r + 1]
    for h in range(heads):
        out[:, h * depth : (h + 1) * depth] = o_buf[:, h, :].astype(bf16)


def attend(queries, new_keys, new_values, key_cache, value_cache, cache_lengths, after):
    count = queries.shape[0]
    return pl.pallas_call(
        lambda *refs: attend_kernel(*refs[:6], *refs[6 + len(after) :]),
        out_shape=jax.ShapeDtypeStruct(queries.shape, queries.dtype),
        in_specs=[SMEM] + [VMEM] * 5 + [ANY] * len(after),
        out_specs=VMEM,
        scratch_shapes=[pltpu.VMEM((count, 8, HEAD_DIM), jnp.float32)] * 2,
        compiler_params=pltpu.CompilerParams(vmem_limit_bytes=8 * 1024 * 1024),
    )(cache_lengths, queries, new_keys, new_values, key_cache, value_cache, *after)


def move_y(value, shift):
    pairs = [
        (z * NY + y, z * NY + (y + shift) % NY) for z in range(NZ) for y in range(NY)
    ]
    return lax.ppermute(value, "grp", pairs)


def move_z(value, shift):
    pairs = [
        (z * NY + y, (z + shift) % NZ * NY + y) for z in range(NZ) for y in range(NY)
    ]
    return lax.ppermute(value, "grp", pairs)


def move_x(value, shift):
    pairs = []
    for x in range(NX):
        pairs.append((x * 2, (x + shift) % NX * 2))
        pairs.append((x * 2 + 1, (x - shift) % NX * 2 + 1))
    return lax.ppermute(value, "tp", pairs)


def swap_core(value):
    return lax.ppermute(value, "tp", [(t, t ^ 1) for t in range(2 * NX)])


def route_kernel(grp, tp, routes_in, gates_in, hidden_in, weights, *rest):
    packed, (routes, gates, hidden, sems) = rest[:EXPERTS], rest[EXPERTS:]
    copies = [
        pltpu.make_async_copy(source, target, sems.at[i])
        for i, (source, target) in enumerate(
            ((routes_in, routes), (gates_in, gates), (hidden_in, hidden))
        )
    ]
    for copy in copies:
        copy.start()
    for copy in copies:
        copy.wait()
    count = hidden.shape[0]
    shape = (EXPERTS * CAP, count)
    line = lax.broadcasted_iota(jnp.int32, shape, 0)
    relative = sum((line >= CAP * r).astype(jnp.int32) for r in range(1, EXPERTS))
    expert = (relative + grp[0]) & (EXPERTS - 1)
    first = routes[0:1, :] == expert
    second = routes[1:2, :] == expert
    member = (first | second).astype(jnp.float32)
    before = lax.broadcasted_iota(jnp.int32, (count, count), 0) < lax.broadcasted_iota(
        jnp.int32, (count, count), 1
    )
    rank = jnp.dot(
        member.astype(jnp.bfloat16),
        before.astype(jnp.float32).astype(jnp.bfloat16),
        preferred_element_type=jnp.float32,
    )
    slot = (line - relative * CAP).astype(jnp.float32)
    place = jnp.where(rank == slot, member, 0.0)
    weights[...] = place * jnp.where(first, gates[0:1, :], gates[1:2, :])
    rows = jnp.dot(
        place.astype(jnp.bfloat16), hidden[...], preferred_element_type=jnp.float32
    )
    for r in range(EXPERTS):
        packed[r][...] = rows[r * CAP : (r + 1) * CAP].astype(jnp.bfloat16)


def route(grp, tp, routes, route_gates, hidden):
    count, width = hidden.shape
    arrays = [routes.T, route_gates.T, hidden]
    return pl.pallas_call(
        route_kernel,
        out_shape=[jax.ShapeDtypeStruct((EXPERTS * CAP, count), jnp.float32)]
        + [jax.ShapeDtypeStruct((CAP, width), jnp.bfloat16)] * EXPERTS,
        in_specs=[SMEM] * 2 + [ANY] * 3,
        out_specs=[VMEM] * (1 + EXPERTS),
        scratch_shapes=[pltpu.VMEM(array.shape, array.dtype) for array in arrays]
        + [pltpu.SemaphoreType.DMA((3,))],
        compiler_params=pltpu.CompilerParams(vmem_limit_bytes=4 * 1024 * 1024),
    )(grp, tp, *[pltpu.with_memory_space_constraint(array, pltpu.HBM) for array in arrays])


def places_of(tp):
    x, c = tp >> 1, tp & 1
    s = 1 - 2 * c

    def block(dx, core):
        return ((x + dx) & (NX - 1)) * 2 + core

    d = 1 - c
    inward = [block(0, c), block(-s, c), block(s, c), block(2, c)]
    inward += [block(0, d), block(s, d), block(-s, d), block(2, d)]
    outward = [block(2, d), block(-s, d), block(s, d), block(0, d)]
    outward += [block(2, c), block(s, c), block(-s, c), block(0, c)]
    return inward, outward


def mlp_kernel(starts, rows, tp, *refs):
    inward, outward = places_of(tp[0])
    count = len(set(ref for ref, _ in starts))
    x_refs, (gain, w_gate, w_up, w_down) = refs[:count], refs[count : count + 4]
    first, second, *keeps = refs[-6:]
    width = x_refs[0].shape[1]

    def block(i):
        ref, start = starts[i]
        return x_refs[ref][start : start + rows, :].astype(jnp.float32)

    squares = None
    for i in range(8):
        x = block(i)
        x = x * x
        part = x[:, 0:128]
        for j in range(1, width // 128):
            part = part + x[:, j * 128 : (j + 1) * 128]
        squares = part if squares is None else squares + part
    mean = jnp.sum(squares, axis=1, keepdims=True) * (1.0 / (8 * width))
    inv_scale = lax.rsqrt(mean + 1e-05)
    gate = up = None
    for i in range(8):
        k = inward[i]
        at = pl.ds(pl.multiple_of(k * width, width), width)
        x = block(i) * inv_scale
        normed = jnp.concatenate(
            [
                x[:, j * 128 : (j + 1) * 128] * gain[pl.ds(k * (width // 128) + j, 1), :]
                for j in range(width // 128)
            ],
            axis=1,
        ).astype(jnp.bfloat16)
        g = jnp.dot(normed, w_gate[at, :], preferred_element_type=jnp.float32)
        u = jnp.dot(normed, w_up[at, :], preferred_element_type=jnp.float32)
        gate, up = (g, u) if i == 0 else (gate + g, up + u)
    act = (gate / (1.0 + jnp.exp(-gate)) * up).astype(jnp.bfloat16)

    def down(i):
        at = pl.ds(pl.multiple_of(outward[i] * width, width), width)
        return jnp.dot(act, w_down[:, at], preferred_element_type=jnp.float32)

    for out, picks in ((first, (0, 2)), (second, (1, 3))):
        for j, pick in enumerate(picks):
            out[j * rows : (j + 1) * rows, :] = down(pick).astype(jnp.bfloat16)
    for j in range(4):
        keeps[j][...] = down(4 + j)


def mlp(tp, xs, rows, gain, w_gate, w_up, w_down, after):
    arrays, starts = [], []
    for array, start in xs:
        same = [i for i, other in enumerate(arrays) if other is array]
        if not same:
            arrays.append(array)
        starts.append((same[0] if same else len(arrays) - 1, start))
    width = arrays[0].shape[1]
    return pl.pallas_call(
        functools.partial(mlp_kernel, tuple(starts), rows),
        out_shape=[
            jax.ShapeDtypeStruct((2 * rows, width), jnp.bfloat16),
            jax.ShapeDtypeStruct((2 * rows, width), jnp.bfloat16),
        ]
        + [jax.ShapeDtypeStruct((rows, width), jnp.float32)] * 4,
        in_specs=[SMEM] + [VMEM] * (len(arrays) + 4) + [ANY] * len(after),
        out_specs=[VMEM] * 6,
        compiler_params=pltpu.CompilerParams(vmem_limit_bytes=VMEM_LIMIT),
    )(tp, *arrays, gain, w_gate, w_up, w_down, *after)


def join_kernel(groups, *refs):
    out, start = refs[-1], 0
    for rows, terms in groups:
        total = None
        for ref, at in terms:
            value = refs[ref][at : at + rows, :]
            if len(terms) > 1:
                value = value.astype(jnp.float32)
            total = value if total is None else total + value
        out[start : start + rows, :] = total.astype(out.dtype)
        start += rows


def join(groups, after=(), hold=()):
    arrays, plan = [], []
    for rows, terms in groups:
        places = []
        for array, at in terms:
            same = [i for i, other in enumerate(arrays) if other is array]
            if not same:
                arrays.append(array)
            places.append((same[0] if same else len(arrays) - 1, at))
        plan.append((rows, tuple(places)))
    total = sum(rows for rows, _ in plan)
    return pl.pallas_call(
        functools.partial(join_kernel, tuple(plan)),
        out_shape=jax.ShapeDtypeStruct((total, arrays[0].shape[1]), jnp.bfloat16),
        in_specs=[VMEM] * (len(arrays) + len(hold)) + [ANY] * len(after),
        out_specs=VMEM,
        compiler_params=pltpu.CompilerParams(vmem_limit_bytes=8 * 1024 * 1024),
    )(*arrays, *hold, *after)


def local(
    queries,
    new_keys,
    new_values,
    key_cache,
    value_cache,
    cache_lengths,
    hidden_b,
    norm_gain,
    routes,
    route_gates,
    w_gate,
    w_up,
    w_down,
):
    bf16, f32 = jnp.bfloat16, jnp.float32
    width = hidden_b.shape[1]
    tp = lax.axis_index("tp").reshape(1)
    gain = norm_gain.reshape(8 * width // 128, 128)
    gate_part, up_part, down_part = w_gate[0], w_up[0], w_down[0]
    weights, *packed = route(
        lax.axis_index("grp").reshape(1), tp, routes, route_gates, hidden_b
    )

    arrived = [packed[0]] + [move_y(packed[r], r) for r in (1, 2, 3)]
    rows_y = lax.optimization_barrier(jnp.concatenate(arrived, axis=0))
    height = rows_y.shape[0]
    by_z = [(0, rows_y)] + [(shift, move_z(rows_y, shift)) for shift in NEAR[1:]]
    z = dict(by_z)

    def experts(xs, rows, after):
        return mlp(tp, xs, rows, gain, gate_part, up_part, down_part, after)

    a, b = len(NEAR) * height, len(FAR) * height
    own_a = join([(height, [(z[shift], 0)]) for shift in NEAR])
    p1_a = move_x(own_a, 1)
    p3_a = move_x(own_a, -1)
    ahead = move_z(join([(height, [(z[1], 0)]), (height, [(z[2], 0)])]), 2)
    behind = move_z(z[-1], -2)
    own_b = join([(2 * height, [(ahead, 0)]), (height, [(behind, 0)])])
    swap_1 = swap_core(join([(a, [(own_a, 0)]), (a, [(p1_a, 0)]), (a, [(p3_a, 0)])], (), [down_part]))
    both_in = join([(a, [(p1_a, 0)]), (b, [(own_b, 0)])], [p3_a])
    both = move_x(both_in, 1)
    p3_b = move_x(own_b, -1)
    attention_a = attend(
        queries, new_keys, new_values, key_cache, value_cache, cache_lengths, [both_in, own_b]
    )
    done = pltpu.with_memory_space_constraint(attention_a, pltpu.HBM)
    p2_in = join([(b, [(both, a)])], [p3_b])
    p2_b = move_x(p2_in, 1)
    swap_3 = swap_core(p2_b)
    swap_2 = swap_core(
        join([(a + b, [(both, 0)]), (b, [(own_b, 0)]), (b, [(p3_b, 0)])], [done, p2_in])
    )

    xs = [(own_a, 0), (p1_a, 0), (p3_a, 0), (both, 0)]
    xs += [(swap_1, 0), (swap_1, a), (swap_1, 2 * a), (swap_2, 0)]
    send_1, send_2, *keep_a = experts(xs, a, [p2_b])
    got_1, got_2a = swap_core(send_1), swap_core(send_2)
    far_a = join([(a, [(keep_a[0], 0), (got_1, 0)])])
    behind_a = join([(a, [(keep_a[2], 0), (got_1, a)])])
    relay_a = move_x(far_a, 1)
    back_a = move_x(behind_a, -1)

    xs = [(own_b, 0), (both, a), (p3_b, 0), (p2_b, 0)]
    xs += [(swap_2, a + b), (swap_2, a), (swap_2, a + 2 * b), (swap_3, 0)]
    send_1, send_2, *keep_b = experts(xs, b, [far_a, behind_a])
    got_1b, got_2b = swap_core(send_1), swap_core(send_2)
    last_a = [(keep_a[1], 0), (got_2a, 0), (relay_a, 0)]
    far_b = join([(b, [(keep_b[0], 0), (got_1b, 0)])])
    both_in = join([(a, last_a)], [back_a, far_b])
    both = move_x(both_in, 1)
    fore_b = move_x(join([(b, [(keep_b[1], 0), (got_2b, 0)])]), 1)
    back_in = join([(b, [(keep_b[2], 0), (got_1b, b)])])
    back_b = move_x(back_in, -1)
    across_b = move_x(join([(b, [(far_b, 0)])], [back_in]), 2)
    mine_a = keep_a[3] + got_2a[a:].astype(f32)
    mine_b = keep_b[3] + got_2b[b:].astype(f32)
    total_a = mine_a + back_a.astype(f32) + both.astype(f32)
    total_b = mine_b + back_b.astype(f32) + fore_b.astype(f32) + across_b.astype(f32)
    returned = {}
    for total, chunk in zip((total_a, total_b), (NEAR, FAR)):
        for i, shift in enumerate(chunk):
            piece = total[i * height : (i + 1) * height]
            if shift == 1:
                terms = [(mine_a, i * height), (back_a, i * height), (both, i * height)]
                piece = join([(height, terms)])
            returned[shift] = piece if shift == 0 else move_z(piece.astype(bf16), -shift).astype(f32)
    summed = returned[0]
    for shift in returned:
        if shift != 0:
            summed = summed + returned[shift]
    rows_back = summed.astype(bf16)
    pieces = [rows_back[r * CAP : (r + 1) * CAP] for r in range(NY)]
    homes = [summed[:CAP]] + [move_y(pieces[r], -r).astype(f32) for r in (1, 2, 3)]
    expert_b = lax.dot_general(
        weights,
        jnp.concatenate(homes, axis=0),
        (((0,), (0,)), ((), ())),
        precision=lax.Precision.HIGHEST,
        preferred_element_type=f32,
    ).astype(bf16)
    return (attention_a, expert_b)


def solution(mesh):
    placed = (
        P("grp", "tp"),
        P("grp", "tp"),
        P("grp", "tp"),
        P("grp", None, "tp"),
        P("grp", None, "tp"),
        P("grp"),
        P("grp", "tp"),
        P(),
        P("grp", None),
        P("grp", None),
        P("grp", None, "tp"),
        P("grp", None, "tp"),
        P("grp", "tp", None),
    )
    return jax.shard_map(
        local,
        mesh=mesh,
        in_specs=placed,
        out_specs=(P("grp", "tp"), P("grp", "tp")),
        check_vma=False,
    )
```

time: 326 us -> 117 us (0.36)
  blocking collectives: 166 us -> 0 us
  waiting for transfers between devices: 90.5 us -> 45.9 us
  starting transfers between devices: 10.4 us -> 52.1 us
  matrix products: 22.8 us -> 0.86 us
  local copies, waits for them, and re-layouts: 18.3 us -> 0.11 us
  Pallas kernels: 0 us -> 13.8 us
  between operations: 14.2 us -> 1.02 us
    all_to_all x1 -> x0, blocking collectives: 153 us -> none  [local(): lax.all_to_all(outgoing, 'grp', split_axis=0, concat_axis=0, tiled=True)]
    reduce_scatter x1 -> x0, waiting for transfers between devices: 56.2 us -> none  [local(): lax.psum_scatter(partial_value, 'tp', scatter_dimension=1, tiled=True)]
    ppermute x0 -> x37, starting transfers between devices: none -> 52.1 us  [the longest x13 27.2 us: move_z(): return lax.ppermute(value, 'grp', pairs)]
    ppermute x0 -> x37, waiting for transfers between devices: none -> 45.9 us  [the longest x11 23.2 us: move_x(): return lax.ppermute(value, 'tp', pairs)]
    all_to_all x1 -> x0, waiting for transfers between devices: 34.4 us -> none  [local(): lax.all_to_all(shares.reshape(groups, capacity, shares.shape[1]), 'grp',...]
    dot_general x7 -> x1, matrix products: 22.8 us -> 0.86 us  [local(): lax.dot_general(weights, jnp.concatenate(homes, axis=0), (((0,), (0,)), (...]
    pallas_call x0 -> x19, Pallas kernels: none -> 13.8 us  [the longest x1 6.41 us: attend(): pl.pallas_call(lambda *refs: attend_kernel(*refs[:6], *refs[6 + len(after...]
    all_gather x1 -> x0, blocking collectives: 13.4 us -> none  [local(): lax.all_gather(hidden_b, 'tp', axis=1, tiled=True).astype(jnp.float32)]
  transfers between devices with their start and end apart: 2 -> 37, of which waited for: 2 -> 16; matrix products, arithmetic and copies ran while one was open for 1% -> 0% of each run, Pallas kernels for 0% -> 8%
where the time goes in v1:
time: 117 us; the launch traced here: 114 us
  starting transfers between devices  52.1 us (45%)
  waiting for transfers between devices  45.9 us (39%)
  Pallas kernels  13.8 us (12%)
    ppermute x13, starting transfers between devices, move_z(): return lax.ppermute(value, 'grp', pairs)  27.2 us
    ppermute x11, waiting for transfers between devices, move_x(): return lax.ppermute(value, 'tp', pairs)  23.2 us
    ppermute x13, waiting for transfers between devices, move_z(): return lax.ppermute(value, 'grp', pairs)  15.2 us
    ppermute x11, starting transfers between devices, move_x(): return lax.ppermute(value, 'tp', pairs)  12.5 us
    ppermute x6, starting transfers between devices, move_y(): return lax.ppermute(value, 'grp', pairs)  10.9 us
    pallas_call x1, Pallas kernels, attend(): pl.pallas_call(lambda *refs: attend_kernel(*refs[:6], *refs[6 + len(after...  6.41 us
    pallas_call x2, Pallas kernels, mlp(): pl.pallas_call(functools.partial(mlp_kernel, tuple(starts), rows), out_sh...  5.39 us
    ppermute x6, waiting for transfers between devices, move_y(): return lax.ppermute(value, 'grp', pairs)  4.65 us
  transfers between devices with their start and end apart: 37, of which 16 were waited for; matrix products, arithmetic and copies ran while one was open for 0% of the time, Pallas kernels for 8%

profile of v1, /device:TPU:8, one launch (start us, length us, event | category | flops | bytes accessed | tf_op | source)
XLA Modules:
  0.0 114.2 jit_solution(11383883599889387996)
XLA Ops:
  0.6 1.2 %shard_map.140 = (f32[48,16]{1,0:T(8,128)S(1)}, bf16[12,768]{1,0:T(8,128)(2,1)S(1)}, bf16[12,768]{1,0:T(8,128)(2,1)S(1)}, bf16[12,768]{1,0:T(8,128)(2,1)S(1)}, bf16[12,768]{1,0:T(8,128)(2,1)S(1)}) custom-call(s32[1]{0:T(128)} %bitcast.grp, s32[1]{0:T(128)} %bitcast.1.tp, s32[2,16]{1,0:T(2,128)} %bitcast.18, f32[2,16]{1,0:T(2,128)} %bitcast.19, ...), custom_call_target="tpu_custom_call" | custom-call | tf_op jit(solution)/shard_map/pallas_call | solution.py:133
  1.9 1.7 %collective-permute-start = (bf16[12,768]{1,0:T(8,128)(2,1)S(1)}, bf16[12,768]{1,0:T(8,128)(2,1)S(1)}, u32[]{:S(2)}, u32[]{:S(2)}) collective-permute-start(bf16[12,768]{1,0:T(8,128)(2,1)S(1)} %get-tuple-element.20), channel_id=1, source_target_pairs={{0,8},{8,16},{16,24},{24,0},{32,40},{40,48},{48,56},{56,32},{64,72... | collective-permute-start | bytes 55304 | tf_op jit(solution)/shard_map/ppermute | solution.py:70
  3.5 2.7 %collective-permute-start.1 = (bf16[12,768]{1,0:T(8,128)(2,1)S(1)}, bf16[12,768]{1,0:T(8,128)(2,1)S(1)}, u32[]{:S(2)}, u32[]{:S(2)}) collective-permute-start(bf16[12,768]{1,0:T(8,128)(2,1)S(1)} %get-tuple-element.21), channel_id=1, source_target_pairs={{0,16},{8,24},{16,0},{24,8},{32,48},{40,56},{48,32},{56,40},{64,80... | collective-permute-start | bytes 55304 | tf_op jit(solution)/shard_map/ppermute | solution.py:70
  6.2 0.7 collective-permute-start.2
  6.9 2.0 %collective-permute-done.1 = bf16[12,768]{1,0:T(8,128)(2,1)S(1)} collective-permute-done((bf16[12,768]{1,0:T(8,128)(2,1)S(1)}, bf16[12,768]{1,0:T(8,128)(2,1)S(1)}, u32[]{:S(2)}, u32[]{:S(2)}) %collective-permute-start.1) | collective-permute-done | bytes 18464 | tf_op jit(solution)/shard_map/ppermute | solution.py:70
  8.9 1.2 %collective-permute-done.2 = bf16[12,768]{1,0:T(8,128)(2,1)S(1)} collective-permute-done((bf16[12,768]{1,0:T(8,128)(2,1)S(1)}, bf16[12,768]{1,0:T(8,128)(2,1)S(1)}, u32[]{:S(2)}, u32[]{:S(2)}) %collective-permute-start.2) | collective-permute-done | bytes 18464 | tf_op jit(solution)/shard_map/ppermute | solution.py:70
  10.1 0.8 collective-permute-start.3
  10.9 4.0 %collective-permute-start.4 = (bf16[48,768]{1,0:T(8,128)(2,1)S(1)}, bf16[48,768]{1,0:T(8,128)(2,1)S(1)}, u32[]{:S(2)}, u32[]{:S(2)}) collective-permute-start(bf16[48,768]{1,0:T(8,128)(2,1)S(1)} %pad_maximum_fusion.refs_0_), channel_id=1, source_target_pairs={{0,224},{8,232},{16,240},{24,248},{32,0},{40,8},{48,16},{56,24},{6... | collective-permute-start | bytes 221192 | tf_op jit(solution)/shard_map/ppermute | solution.py:77
  14.9 4.1 %collective-permute-start.6 = (bf16[48,768]{1,0:T(8,128)(2,1)S(1)}, bf16[48,768]{1,0:T(8,128)(2,1)S(1)}, u32[]{:S(2)}, u32[]{:S(2)}) collective-permute-start(bf16[48,768]{1,0:T(8,128)(2,1)S(1)} %pad_maximum_fusion.refs_0_), channel_id=1, source_target_pairs={{0,192},{8,200},{16,208},{24,216},{32,224},{40,232},{48,240},{56,2... | collective-permute-start | bytes 221192 | tf_op jit(solution)/shard_map/ppermute | solution.py:77
  19.1 2.9 %collective-permute-done.5.refs_3_.refs_1_ = bf16[48,768]{1,0:T(8,128)(2,1)S(1)} collective-permute-done((bf16[48,768]{1,0:T(8,128)(2,1)S(1)}, bf16[48,768]{1,0:T(8,128)(2,1)S(1)}, u32[]{:S(2)}, u32[]{:S(2)}) %collective-permute-start.5) | collective-permute-done | bytes 73760 | tf_op jit(solution)/shard_map/ppermute | solution.py:77
  21.9 0.8 collective-permute-done.6.refs_4_
  22.8 2.8 %collective-permute-start.10 = (bf16[240,768]{1,0:T(8,128)(2,1)S(1)}, bf16[240,768]{1,0:T(8,128)(2,1)S(1)}, u32[]{:S(2)}, u32[]{:S(2)}) collective-permute-start(bf16[240,768]{1,0:T(8,128)(2,1)S(1)} %shard_map.141.refs_0_), channel_id=1, source_target_pairs={{0,6},{1,3},{2,0},{3,5},{4,2},{5,7},{6,4},{7,1},{8,14},{9,11},{10,... | collective-permute-start | bytes 1105928 | tf_op jit(solution)/shard_map/ppermute | solution.py:85
  25.7 3.8 %collective-permute-start.8 = (bf16[96,768]{1,0:T(8,128)(2,1)S(1)}, bf16[96,768]{1,0:T(8,128)(2,1)S(1)}, u32[]{:S(2)}, u32[]{:S(2)}) collective-permute-start(bf16[96,768]{1,0:T(8,128)(2,1)S(1)} %shard_map.142), channel_id=1, source_target_pairs={{0,64},{8,72},{16,80},{24,88},{32,96},{40,104},{48,112},{56,120},{... | collective-permute-start | bytes 442376 | tf_op jit(solution)/shard_map/ppermute | solution.py:77
  29.5 0.4 collective-permute-start.9
  29.9 5.1 %collective-permute-done.9.refs_1_ = bf16[48,768]{1,0:T(8,128)(2,1)S(1)} collective-permute-done((bf16[48,768]{1,0:T(8,128)(2,1)S(1)}, bf16[48,768]{1,0:T(8,128)(2,1)S(1)}, u32[]{:S(2)}, u32[]{:S(2)}) %collective-permute-start.9) | collective-permute-done | bytes 73760 | tf_op jit(solution)/shard_map/ppermute | solution.py:77
  35.2 0.8 collective-permute-start.11
  36.0 2.6 %collective-permute-start.13 = (bf16[144,768]{1,0:T(8,128)(2,1)S(1)}, bf16[144,768]{1,0:T(8,128)(2,1)S(1)}, u32[]{:S(2)}, u32[]{:S(2)}) collective-permute-start(bf16[144,768]{1,0:T(8,128)(2,1)S(1)} %shard_map.143.refs_1_.refs_7_.refs_0_), channel_id=1, source_target_pairs={{0,6},{1,3},{2,0},{3,5},{4,2},{5,7},{6,4},{7,1},{8,14},{9,11},{10,... | collective-permute-start | bytes 663560 | tf_op jit(solution)/shard_map/ppermute | solution.py:85
  38.6 0.1 shard_map.146
  38.7 0.1 collective-permute-start.12
  38.8 6.4 %shard_map.145.refs_3_ = bf16[16,768]{1,0:T(8,128)(2,1)} custom-call(s32[16]{0:T(128)S(1)} %copy-done.9, bf16[16,768]{1,0:T(8,128)(2,1)S(1)} %copy-done.6, bf16[16,128]{1,0:T(8,128)(2,1)S(1)} %copy-done.7, bf16[16,128]{1,0:T(8,128)(2,1)S(1)} %copy-done.8, bf16[16,256,128]{2,1,0:T(8,128)(2,1)S(1)} %copy-done.3, bf16[16,256,128]{2,1,0:T(8,128)(2,1)S(1)} %copy-done.4, ...), custom_call_target="tpu_custom_call" | custom-call | tf_op jit(solution)/shard_map/pallas_call | solution.py:56
  45.3 1.1 collective-permute-done.11.refs_0_.refs_3_.refs_1_
  46.4 0.1 shard_map.148
  46.4 0.1 collective-permute-start.14
  46.5 0.3 collective-permute-start.15
  46.8 7.1 %collective-permute-done.15.refs_10_.refs_3_ = bf16[144,768]{1,0:T(8,128)(2,1)S(1)} collective-permute-done((bf16[144,768]{1,0:T(8,128)(2,1)S(1)}, bf16[144,768]{1,0:T(8,128)(2,1)S(1)}, u32[]{:S(2)}, u32[]{:S(2)}) %collective-permute-start.15) | collective-permute-done | bytes 221216 | tf_op jit(solution)/shard_map/ppermute | solution.py:85
  54.0 3.2 %shard_map.149 = (bf16[480,768]{1,0:T(8,128)(2,1)S(1)}, bf16[480,768]{1,0:T(8,128)(2,1)S(1)}, f32[240,768]{1,0:T(8,128)S(1)}, f32[240,768]{1,0:T(8,128)S(1)}, f3...) custom-call(s32[1]{0:T(128)} %bitcast.1.tp, bf16[240,768]{1,0:T(8,128)(2,1)S(1)} %shard_map.141.refs_0_, ...), custom_call_target="tpu_custom_call" | custom-call | tf_op jit(solution)/shard_map/pallas_call | solution.py:217
  57.2 0.1 collective-permute-start.17
  57.3 0.5 collective-permute-start.16
  57.8 0.1 collective-permute-start.20
  57.9 1.6 %collective-permute-done.17.refs_1_ = bf16[480,768]{1,0:T(8,128)(2,1)S(1)} collective-permute-done((bf16[480,768]{1,0:T(8,128)(2,1)S(1)}, bf16[480,768]{1,0:T(8,128)(2,1)S(1)}, u32[]{:S(2)}, u32[]{:S(2)}) %collective-permute-start.17) | collective-permute-done | bytes 737312 | tf_op jit(solution)/shard_map/ppermute | solution.py:89
  59.5 0.1 shard_map.150.refs_11_
  59.6 0.1 shard_map.151.refs_10_
  59.6 1.2 %collective-permute-done.20.refs_5_ = bf16[144,768]{1,0:T(8,128)(2,1)S(1)} collective-permute-done((bf16[144,768]{1,0:T(8,128)(2,1)S(1)}, bf16[144,768]{1,0:T(8,128)(2,1)S(1)}, u32[]{:S(2)}, u32[]{:S(2)}) %collective-permute-start.20) | collective-permute-done | bytes 221216 | tf_op jit(solution)/shard_map/ppermute | solution.py:89
  60.9 2.2 %shard_map.152 = (bf16[288,768]{1,0:T(8,128)(2,1)S(1)}, bf16[288,768]{1,0:T(8,128)(2,1)S(1)}, f32[144,768]{1,0:T(8,128)S(1)}, f32[144,768]{1,0:T(8,128)S(1)}, f3...) custom-call(s32[1]{0:T(128)} %bitcast.1.tp, bf16[144,768]{1,0:T(8,128)(2,1)S(1)} %shard_map.143.refs_1_.refs_7_.refs_0_, ...), custom_call_target="tpu_custom_call" | custom-call | tf_op jit(solution)/shard_map/pallas_call | solution.py:217
  63.1 0.2 collective-permute-start.27
  63.3 0.4 collective-permute-start.21
  63.7 0.8 collective-permute-start.18
  64.5 1.2 %collective-permute-start.19 = (bf16[240,768]{1,0:T(8,128)(2,1)S(1)}, bf16[240,768]{1,0:T(8,128)(2,1)S(1)}, u32[]{:S(2)}, u32[]{:S(2)}) collective-permute-start(bf16[240,768]{1,0:T(8,128)(2,1)S(1)} %shard_map.151.refs_10_), channel_id=1, source_target_pairs={{0,2},{1,7},{2,4},{3,1},{4,6},{5,3},{6,0},{7,5},{8,10},{9,15},{10,... | collective-permute-start | bytes 1105928 | tf_op jit(solution)/shard_map/ppermute | solution.py:85
  65.7 0.1 collective-permute-start.29
  65.9 0.1 shard_map.156.refs_1_
  66.0 3.6 %collective-permute-start.30 = (bf16[144,768]{1,0:T(8,128)(2,1)S(1)}, bf16[144,768]{1,0:T(8,128)(2,1)S(1)}, u32[]{:S(2)}, u32[]{:S(2)}) collective-permute-start(bf16[144,768]{1,0:T(8,128)(2,1)S(1)} %shard_map.158), channel_id=1, source_target_pairs={{0,4},{1,5},{2,6},{3,7},{4,0},{5,1},{6,2},{7,3},{8,12},{9,13},{10,... | collective-permute-start | bytes 663560 | tf_op jit(solution)/shard_map/ppermute | solution.py:85
  69.5 5.5 %collective-permute-done.18.refs_3_.refs_1_ = bf16[240,768]{1,0:T(8,128)(2,1)S(1)} collective-permute-done((bf16[240,768]{1,0:T(8,128)(2,1)S(1)}, bf16[240,768]{1,0:T(8,128)(2,1)S(1)}, u32[]{:S(2)}, u32[]{:S(2)}) %collective-permute-start.18) | collective-permute-done | bytes 368672 | tf_op jit(solution)/shard_map/ppermute | solution.py:85
  75.1 4.5 %collective-permute-done.19.refs_2_ = bf16[240,768]{1,0:T(8,128)(2,1)S(1)} collective-permute-done((bf16[240,768]{1,0:T(8,128)(2,1)S(1)}, bf16[240,768]{1,0:T(8,128)(2,1)S(1)}, u32[]{:S(2)}, u32[]{:S(2)}) %collective-permute-start.19) | collective-permute-done | bytes 368672 | tf_op jit(solution)/shard_map/ppermute | solution.py:85
  79.6 0.2 shard_map.154
  79.8 0.3 collective-permute-start.22
  80.1 4.9 %collective-permute-done.29 = bf16[144,768]{1,0:T(8,128)(2,1)S(1)} collective-permute-done((bf16[144,768]{1,0:T(8,128)(2,1)S(1)}, bf16[144,768]{1,0:T(8,128)(2,1)S(1)}, u32[]{:S(2)}, u32[]{:S(2)}) %collective-permute-start.29) | collective-permute-done | bytes 221216 | tf_op jit(solution)/shard_map/ppermute | solution.py:85
  85.0 0.1 add_convert_fusion
  85.2 1.8 %collective-permute-start.31 = (bf16[48,768]{1,0:T(8,128)(2,1)S(1)}, bf16[48,768]{1,0:T(8,128)(2,1)S(1)}, u32[]{:S(2)}, u32[]{:S(2)}) collective-permute-start(bf16[48,768]{1,0:T(8,128)(2,1)S(1)} %get-tuple-element.44), channel_id=1, source_target_pairs={{0,160},{8,168},{16,176},{24,184},{32,192},{40,200},{48,208},{56,2... | collective-permute-start | bytes 221192 | tf_op jit(solution)/shard_map/ppermute | solution.py:77
  86.9 2.5 %collective-permute-start.32 = (bf16[48,768]{1,0:T(8,128)(2,1)S(1)}, bf16[48,768]{1,0:T(8,128)(2,1)S(1)}, u32[]{:S(2)}, u32[]{:S(2)}) collective-permute-start(bf16[48,768]{1,0:T(8,128)(2,1)S(1)} %get-tuple-element.46), channel_id=1, source_target_pairs={{0,128},{8,136},{16,144},{24,152},{32,160},{40,168},{48,176},{56,1... | collective-permute-start | bytes 221192 | tf_op jit(solution)/shard_map/ppermute | solution.py:77
  89.5 2.2 %collective-permute-start.33 = (bf16[48,768]{1,0:T(8,128)(2,1)S(1)}, bf16[48,768]{1,0:T(8,128)(2,1)S(1)}, u32[]{:S(2)}, u32[]{:S(2)}) collective-permute-start(bf16[48,768]{1,0:T(8,128)(2,1)S(1)} %get-tuple-element.45), channel_id=1, source_target_pairs={{0,96},{8,104},{16,112},{24,120},{32,128},{40,136},{48,144},{56,15... | collective-permute-start | bytes 221192 | tf_op jit(solution)/shard_map/ppermute | solution.py:77
  91.7 0.2 fusion.16
  91.9 3.8 %collective-permute-start.23 = (bf16[48,768]{1,0:T(8,128)(2,1)S(1)}, bf16[48,768]{1,0:T(8,128)(2,1)S(1)}, u32[]{:S(2)}, u32[]{:S(2)}) collective-permute-start(bf16[48,768]{1,0:T(8,128)(2,1)S(1)} %shard_map.155), channel_id=1, source_target_pairs={{0,224},{8,232},{16,240},{24,248},{32,0},{40,8},{48,16},{56,24},{6... | collective-permute-start | bytes 221192 | tf_op jit(solution)/shard_map/ppermute | solution.py:77
  95.7 0.1 collective-permute-start.24
  95.8 3.4 %collective-permute-start.25 = (bf16[48,768]{1,0:T(8,128)(2,1)S(1)}, bf16[48,768]{1,0:T(8,128)(2,1)S(1)}, u32[]{:S(2)}, u32[]{:S(2)}) collective-permute-start(bf16[48,768]{1,0:T(8,128)(2,1)S(1)} %get-tuple-element.43), channel_id=1, source_target_pairs={{0,192},{8,200},{16,208},{24,216},{32,224},{40,232},{48,240},{56,2... | collective-permute-start | bytes 221192 | tf_op jit(solution)/shard_map/ppermute | solution.py:77
  99.2 0.2 collective-permute-start.26
  99.4 3.5 %collective-permute-done.24 = bf16[48,768]{1,0:T(8,128)(2,1)S(1)} collective-permute-done((bf16[48,768]{1,0:T(8,128)(2,1)S(1)}, bf16[48,768]{1,0:T(8,128)(2,1)S(1)}, u32[]{:S(2)}, u32[]{:S(2)}) %collective-permute-start.24) | collective-permute-done | bytes 73760 | tf_op jit(solution)/shard_map/ppermute | solution.py:77
  102.9 2.8 %collective-permute-done.26 = bf16[48,768]{1,0:T(8,128)(2,1)S(1)} collective-permute-done((bf16[48,768]{1,0:T(8,128)(2,1)S(1)}, bf16[48,768]{1,0:T(8,128)(2,1)S(1)}, u32[]{:S(2)}, u32[]{:S(2)}) %collective-permute-start.26) | collective-permute-done | bytes 73760 | tf_op jit(solution)/shard_map/ppermute | solution.py:77
  105.8 0.1 fusion.14
  105.9 1.9 %collective-permute-start.34 = (bf16[12,768]{1,0:T(8,128)(2,1)S(1)}, bf16[12,768]{1,0:T(8,128)(2,1)S(1)}, u32[]{:S(2)}, u32[]{:S(2)}) collective-permute-start(bf16[12,768]{1,0:T(8,128)(2,1)S(1)} %get-tuple-element.47), channel_id=1, source_target_pairs={{0,24},{8,0},{16,8},{24,16},{32,56},{40,32},{48,40},{56,48},{64,88... | collective-permute-start | bytes 55304 | tf_op jit(solution)/shard_map/ppermute | solution.py:70
  107.8 1.5 %collective-permute-start.35 = (bf16[12,768]{1,0:T(8,128)(2,1)S(1)}, bf16[12,768]{1,0:T(8,128)(2,1)S(1)}, u32[]{:S(2)}, u32[]{:S(2)}) collective-permute-start(bf16[12,768]{1,0:T(8,128)(2,1)S(1)} %get-tuple-element.49), channel_id=1, source_target_pairs={{0,16},{8,24},{16,0},{24,8},{32,48},{40,56},{48,32},{56,40},{64,80... | collective-permute-start | bytes 55304 | tf_op jit(solution)/shard_map/ppermute | solution.py:70
  109.3 2.5 %collective-permute-start.36 = (bf16[12,768]{1,0:T(8,128)(2,1)S(1)}, bf16[12,768]{1,0:T(8,128)(2,1)S(1)}, u32[]{:S(2)}, u32[]{:S(2)}) collective-permute-start(bf16[12,768]{1,0:T(8,128)(2,1)S(1)} %get-tuple-element.48), channel_id=1, source_target_pairs={{0,8},{8,16},{16,24},{24,0},{32,40},{40,48},{48,56},{56,32},{64,72... | collective-permute-start | bytes 55304 | tf_op jit(solution)/shard_map/ppermute | solution.py:70
  111.8 1.3 %collective-permute-done.35 = bf16[12,768]{1,0:T(8,128)(2,1)S(1)} collective-permute-done((bf16[12,768]{1,0:T(8,128)(2,1)S(1)}, bf16[12,768]{1,0:T(8,128)(2,1)S(1)}, u32[]{:S(2)}, u32[]{:S(2)}) %collective-permute-start.35) | collective-permute-done | bytes 18464 | tf_op jit(solution)/shard_map/ppermute | solution.py:70
  113.1 0.2 collective-permute-done.36
  113.3 0.9 convolution_convert_fusion
  (61 shorter events, 0.5 us)
Async XLA Ops:
  0.6 37.9 %copy-start = (bf16[1,256,6144]{2,1,0:T(8,128)(2,1)S(1)}, bf16[1,256,6144]{2,1,0:T(8,128)(2,1)}, u32[]{:S(2)}) copy-start(bf16[1,256,6144]{2,1,0:T(8,128)(2,1)} %param.25) | copy-start | bytes 9437188
  1.9 5.0 %collective-permute-start = (bf16[12,768]{1,0:T(8,128)(2,1)S(1)}, bf16[12,768]{1,0:T(8,128)(2,1)S(1)}, u32[]{:S(2)}, u32[]{:S(2)}) collective-permute-start(bf16[12,768]{1,0:T(8,128)(2,1)S(1)} %get-tuple-element.20), channel_id=1, source_target_pairs={{0,8},{8,16},{16,24},{24,0},{32,40},{40,48},{48,56},{56,32},{64,72... | collective-permute-start | bytes 55304 | tf_op jit(solution)/shard_map/ppermute | solution.py:70
  3.5 5.3 %collective-permute-start.1 = (bf16[12,768]{1,0:T(8,128)(2,1)S(1)}, bf16[12,768]{1,0:T(8,128)(2,1)S(1)}, u32[]{:S(2)}, u32[]{:S(2)}) collective-permute-start(bf16[12,768]{1,0:T(8,128)(2,1)S(1)} %get-tuple-element.21), channel_id=1, source_target_pairs={{0,16},{8,24},{16,0},{24,8},{32,48},{40,56},{48,32},{56,40},{64,80... | collective-permute-start | bytes 55304 | tf_op jit(solution)/shard_map/ppermute | solution.py:70
  6.2 3.8 %collective-permute-start.2 = (bf16[12,768]{1,0:T(8,128)(2,1)S(1)}, bf16[12,768]{1,0:T(8,128)(2,1)S(1)}, u32[]{:S(2)}, u32[]{:S(2)}) collective-permute-start(bf16[12,768]{1,0:T(8,128)(2,1)S(1)} %get-tuple-element.22), channel_id=1, source_target_pairs={{0,24},{8,0},{16,8},{24,16},{32,56},{40,32},{48,40},{56,48},{64,88... | collective-permute-start | bytes 55304 | tf_op jit(solution)/shard_map/ppermute | solution.py:70
  10.1 9.0 %collective-permute-start.3 = (bf16[48,768]{1,0:T(8,128)(2,1)S(1)}, bf16[48,768]{1,0:T(8,128)(2,1)S(1)}, u32[]{:S(2)}, u32[]{:S(2)}) collective-permute-start(bf16[48,768]{1,0:T(8,128)(2,1)S(1)} %pad_maximum_fusion.refs_0_), channel_id=1, source_target_pairs={{0,32},{8,40},{16,48},{24,56},{32,64},{40,72},{48,80},{56,88},{64,... | collective-permute-start | bytes 221192 | tf_op jit(solution)/shard_map/ppermute | solution.py:77
  10.9 8.2 %collective-permute-start.4 = (bf16[48,768]{1,0:T(8,128)(2,1)S(1)}, bf16[48,768]{1,0:T(8,128)(2,1)S(1)}, u32[]{:S(2)}, u32[]{:S(2)}) collective-permute-start(bf16[48,768]{1,0:T(8,128)(2,1)S(1)} %pad_maximum_fusion.refs_0_), channel_id=1, source_target_pairs={{0,224},{8,232},{16,240},{24,248},{32,0},{40,8},{48,16},{56,24},{6... | collective-permute-start | bytes 221192 | tf_op jit(solution)/shard_map/ppermute | solution.py:77
  14.9 7.0 %collective-permute-start.5 = (bf16[48,768]{1,0:T(8,128)(2,1)S(1)}, bf16[48,768]{1,0:T(8,128)(2,1)S(1)}, u32[]{:S(2)}, u32[]{:S(2)}) collective-permute-start(bf16[48,768]{1,0:T(8,128)(2,1)S(1)} %pad_maximum_fusion.refs_0_), channel_id=1, source_target_pairs={{0,64},{8,72},{16,80},{24,88},{32,96},{40,104},{48,112},{56,120},{... | collective-permute-start | bytes 221192 | tf_op jit(solution)/shard_map/ppermute | solution.py:77
  14.9 7.9 %collective-permute-start.6 = (bf16[48,768]{1,0:T(8,128)(2,1)S(1)}, bf16[48,768]{1,0:T(8,128)(2,1)S(1)}, u32[]{:S(2)}, u32[]{:S(2)}) collective-permute-start(bf16[48,768]{1,0:T(8,128)(2,1)S(1)} %pad_maximum_fusion.refs_0_), channel_id=1, source_target_pairs={{0,192},{8,200},{16,208},{24,216},{32,224},{40,232},{48,240},{56,2... | collective-permute-start | bytes 221192 | tf_op jit(solution)/shard_map/ppermute | solution.py:77
  22.8 12.3 %collective-permute-start.10 = (bf16[240,768]{1,0:T(8,128)(2,1)S(1)}, bf16[240,768]{1,0:T(8,128)(2,1)S(1)}, u32[]{:S(2)}, u32[]{:S(2)}) collective-permute-start(bf16[240,768]{1,0:T(8,128)(2,1)S(1)} %shard_map.141.refs_0_), channel_id=1, source_target_pairs={{0,6},{1,3},{2,0},{3,5},{4,2},{5,7},{6,4},{7,1},{8,14},{9,11},{10,... | collective-permute-start | bytes 1105928 | tf_op jit(solution)/shard_map/ppermute | solution.py:85
  25.6 9.5 %collective-permute-start.7 = (bf16[240,768]{1,0:T(8,128)(2,1)S(1)}, bf16[240,768]{1,0:T(8,128)(2,1)S(1)}, u32[]{:S(2)}, u32[]{:S(2)}) collective-permute-start(bf16[240,768]{1,0:T(8,128)(2,1)S(1)} %shard_map.141.refs_0_), channel_id=1, source_target_pairs={{0,2},{1,7},{2,4},{3,1},{4,6},{5,3},{6,0},{7,5},{8,10},{9,15},{10,... | collective-permute-start | bytes 1105928 | tf_op jit(solution)/shard_map/ppermute | solution.py:85
  25.7 9.4 %collective-permute-start.8 = (bf16[96,768]{1,0:T(8,128)(2,1)S(1)}, bf16[96,768]{1,0:T(8,128)(2,1)S(1)}, u32[]{:S(2)}, u32[]{:S(2)}) collective-permute-start(bf16[96,768]{1,0:T(8,128)(2,1)S(1)} %shard_map.142), channel_id=1, source_target_pairs={{0,64},{8,72},{16,80},{24,88},{32,96},{40,104},{48,112},{56,120},{... | collective-permute-start | bytes 442376 | tf_op jit(solution)/shard_map/ppermute | solution.py:77
  29.5 5.5 %collective-permute-start.9 = (bf16[48,768]{1,0:T(8,128)(2,1)S(1)}, bf16[48,768]{1,0:T(8,128)(2,1)S(1)}, u32[]{:S(2)}, u32[]{:S(2)}) collective-permute-start(bf16[48,768]{1,0:T(8,128)(2,1)S(1)} %collective-permute-done.4.refs_2_), channel_id=1, source_target_pairs={{0,192},{8,200},{16,208},{24,216},{32,224},{40,232},{48,240},{56,2... | collective-permute-start | bytes 221192 | tf_op jit(solution)/shard_map/ppermute | solution.py:77
  35.0 3.8 %copy-start.3 = (bf16[16,256,128]{2,1,0:T(8,128)(2,1)S(1)}, bf16[16,256,128]{2,1,0:T(8,128)(2,1)}, u32[]{:S(2)}) copy-start(bf16[16,256,128]{2,1,0:T(8,128)(2,1)} %refs_4_.1) | copy-start | bytes 3145732
  35.0 3.7 %copy-start.4 = (bf16[16,256,128]{2,1,0:T(8,128)(2,1)S(1)}, bf16[16,256,128]{2,1,0:T(8,128)(2,1)}, u32[]{:S(2)}) copy-start(bf16[16,256,128]{2,1,0:T(8,128)(2,1)} %refs_5_.1) | copy-start | bytes 3145732
  35.1 3.7 %copy-start.6 = (bf16[16,768]{1,0:T(8,128)(2,1)S(1)}, bf16[16,768]{1,0:T(8,128)(2,1)}, u32[]{:S(2)}) copy-start(bf16[16,768]{1,0:T(8,128)(2,1)} %refs_1_.1) | copy-start | bytes 73732
  35.1 3.7 %copy-start.7 = (bf16[16,128]{1,0:T(8,128)(2,1)S(1)}, bf16[16,128]{1,0:T(8,128)(2,1)}, u32[]{:S(2)}) copy-start(bf16[16,128]{1,0:T(8,128)(2,1)} %refs_2_.1) | copy-start | bytes 12292
  35.1 3.7 %copy-start.8 = (bf16[16,128]{1,0:T(8,128)(2,1)S(1)}, bf16[16,128]{1,0:T(8,128)(2,1)}, u32[]{:S(2)}) copy-start(bf16[16,128]{1,0:T(8,128)(2,1)} %refs_3_.1) | copy-start | bytes 12292
  35.1 3.7 %copy-start.9 = (s32[16]{0:T(128)S(1)}, s32[16]{0:T(128)}, u32[]{:S(2)}) copy-start(s32[16]{0:T(128)} %refs_0_.1) | copy-start | bytes 196
  35.2 11.2 %collective-permute-start.11 = (bf16[384,768]{1,0:T(8,128)(2,1)S(1)}, bf16[384,768]{1,0:T(8,128)(2,1)S(1)}, u32[]{:S(2)}, u32[]{:S(2)}) collective-permute-start(bf16[384,768]{1,0:T(8,128)(2,1)S(1)} %shard_map.144.refs_6_), channel_id=1, source_target_pairs={{0,2},{1,7},{2,4},{3,1},{4,6},{5,3},{6,0},{7,5},{8,10},{9,15},{10,... | collective-permute-start | bytes 1769480 | tf_op jit(solution)/shard_map/ppermute | solution.py:85
  36.0 9.2 %collective-permute-start.13 = (bf16[144,768]{1,0:T(8,128)(2,1)S(1)}, bf16[144,768]{1,0:T(8,128)(2,1)S(1)}, u32[]{:S(2)}, u32[]{:S(2)}) collective-permute-start(bf16[144,768]{1,0:T(8,128)(2,1)S(1)} %shard_map.143.refs_1_.refs_7_.refs_0_), channel_id=1, source_target_pairs={{0,6},{1,3},{2,0},{3,5},{4,2},{5,7},{6,4},{7,1},{8,14},{9,11},{10,... | collective-permute-start | bytes 663560 | tf_op jit(solution)/shard_map/ppermute | solution.py:85
  38.6 15.4 %copy-start.5 = (f32[6144]{0:T(1024)S(1)}, f32[6144]{0:T(1024)}, u32[]{:S(2)}) copy-start(f32[6144]{0:T(1024)} %param.20) | copy-start | bytes 73732
  38.7 15.3 %copy-start.1 = (bf16[1,6144,256]{2,1,0:T(8,128)(2,1)S(1)}, bf16[1,6144,256]{2,1,0:T(8,128)(2,1)}, u32[]{:S(2)}) copy-start(bf16[1,6144,256]{2,1,0:T(8,128)(2,1)} %param.23) | copy-start | bytes 9437188
  38.7 15.3 %copy-start.2 = (bf16[1,6144,256]{2,1,0:T(8,128)(2,1)S(1)}, bf16[1,6144,256]{2,1,0:T(8,128)(2,1)}, u32[]{:S(2)}) copy-start(bf16[1,6144,256]{2,1,0:T(8,128)(2,1)} %param.24) | copy-start | bytes 9437188
  38.7 15.3 %collective-permute-start.12 = (bf16[720,768]{1,0:T(8,128)(2,1)S(1)}, bf16[720,768]{1,0:T(8,128)(2,1)S(1)}, u32[]{:S(2)}, u32[]{:S(2)}) collective-permute-start(bf16[720,768]{1,0:T(8,128)(2,1)S(1)} %shard_map.146), channel_id=1, source_target_pairs={{0,1},{1,0},{2,3},{3,2},{4,5},{5,4},{6,7},{7,6},{8,9},{9,8},{10,11... | collective-permute-start | bytes 3317768 | tf_op jit(solution)/shard_map/ppermute | solution.py:89
  46.4 7.5 %collective-permute-start.14 = (bf16[672,768]{1,0:T(8,128)(2,1)S(1)}, bf16[672,768]{1,0:T(8,128)(2,1)S(1)}, u32[]{:S(2)}, u32[]{:S(2)}) collective-permute-start(bf16[672,768]{1,0:T(8,128)(2,1)S(1)} %shard_map.148), channel_id=1, source_target_pairs={{0,1},{1,0},{2,3},{3,2},{4,5},{5,4},{6,7},{7,6},{8,9},{9,8},{10,11... | collective-permute-start | bytes 3096584 | tf_op jit(solution)/shard_map/ppermute | solution.py:89
  46.5 7.4 %collective-permute-start.15 = (bf16[144,768]{1,0:T(8,128)(2,1)S(1)}, bf16[144,768]{1,0:T(8,128)(2,1)S(1)}, u32[]{:S(2)}, u32[]{:S(2)}) collective-permute-start(bf16[144,768]{1,0:T(8,128)(2,1)S(1)} %shard_map.147.refs_4_), channel_id=1, source_target_pairs={{0,2},{1,7},{2,4},{3,1},{4,6},{5,3},{6,0},{7,5},{8,10},{9,15},{10,... | collective-permute-start | bytes 663560 | tf_op jit(solution)/shard_map/ppermute | solution.py:85
  57.2 2.3 %collective-permute-start.17 = (bf16[480,768]{1,0:T(8,128)(2,1)S(1)}, bf16[480,768]{1,0:T(8,128)(2,1)S(1)}, u32[]{:S(2)}, u32[]{:S(2)}) collective-permute-start(bf16[480,768]{1,0:T(8,128)(2,1)S(1)} %get-tuple-element.27), channel_id=1, source_target_pairs={{0,1},{1,0},{2,3},{3,2},{4,5},{5,4},{6,7},{7,6},{8,9},{9,8},{10,11... | collective-permute-start | bytes 2211848 | tf_op jit(solution)/shard_map/ppermute | solution.py:89
  57.3 12.3 %collective-permute-start.16 = (bf16[480,768]{1,0:T(8,128)(2,1)S(1)}, bf16[480,768]{1,0:T(8,128)(2,1)S(1)}, u32[]{:S(2)}, u32[]{:S(2)}) collective-permute-start(bf16[480,768]{1,0:T(8,128)(2,1)S(1)} %get-tuple-element.25), channel_id=1, source_target_pairs={{0,1},{1,0},{2,3},{3,2},{4,5},{5,4},{6,7},{7,6},{8,9},{9,8},{10,11... | collective-permute-start | bytes 2211848 | tf_op jit(solution)/shard_map/ppermute | solution.py:89
  57.8 3.1 %collective-permute-start.20 = (bf16[144,768]{1,0:T(8,128)(2,1)S(1)}, bf16[144,768]{1,0:T(8,128)(2,1)S(1)}, u32[]{:S(2)}, u32[]{:S(2)}) collective-permute-start(bf16[144,768]{1,0:T(8,128)(2,1)S(1)} %collective-permute-done.15.refs_10_.refs_3_), channel_id=1, source_target_pairs={{0,1},{1,0},{2,3},{3,2},{4,5},{5,4},{6,7},{7,6},{8,9},{9,8},{10,11... | collective-permute-start | bytes 663560 | tf_op jit(solution)/shard_map/ppermute | solution.py:89
  63.1 2.6 %collective-permute-start.27 = (bf16[288,768]{1,0:T(8,128)(2,1)S(1)}, bf16[288,768]{1,0:T(8,128)(2,1)S(1)}, u32[]{:S(2)}, u32[]{:S(2)}) collective-permute-start(bf16[288,768]{1,0:T(8,128)(2,1)S(1)} %get-tuple-element.33), channel_id=1, source_target_pairs={{0,1},{1,0},{2,3},{3,2},{4,5},{5,4},{6,7},{7,6},{8,9},{9,8},{10,11... | collective-permute-start | bytes 1327112 | tf_op jit(solution)/shard_map/ppermute | solution.py:89
  63.3 2.5 %collective-permute-start.21 = (bf16[288,768]{1,0:T(8,128)(2,1)S(1)}, bf16[288,768]{1,0:T(8,128)(2,1)S(1)}, u32[]{:S(2)}, u32[]{:S(2)}) collective-permute-start(bf16[288,768]{1,0:T(8,128)(2,1)S(1)} %get-tuple-element.31), channel_id=1, source_target_pairs={{0,1},{1,0},{2,3},{3,2},{4,5},{5,4},{6,7},{7,6},{8,9},{9,8},{10,11... | collective-permute-start | bytes 1327112 | tf_op jit(solution)/shard_map/ppermute | solution.py:89
  63.7 11.4 %collective-permute-start.18 = (bf16[240,768]{1,0:T(8,128)(2,1)S(1)}, bf16[240,768]{1,0:T(8,128)(2,1)S(1)}, u32[]{:S(2)}, u32[]{:S(2)}) collective-permute-start(bf16[240,768]{1,0:T(8,128)(2,1)S(1)} %shard_map.150.refs_11_), channel_id=1, source_target_pairs={{0,6},{1,3},{2,0},{3,5},{4,2},{5,7},{6,4},{7,1},{8,14},{9,11},{10,... | collective-permute-start | bytes 1105928 | tf_op jit(solution)/shard_map/ppermute | solution.py:85
  64.5 15.1 %collective-permute-start.19 = (bf16[240,768]{1,0:T(8,128)(2,1)S(1)}, bf16[240,768]{1,0:T(8,128)(2,1)S(1)}, u32[]{:S(2)}, u32[]{:S(2)}) collective-permute-start(bf16[240,768]{1,0:T(8,128)(2,1)S(1)} %shard_map.151.refs_10_), channel_id=1, source_target_pairs={{0,2},{1,7},{2,4},{3,1},{4,6},{5,3},{6,0},{7,5},{8,10},{9,15},{10,... | collective-permute-start | bytes 1105928 | tf_op jit(solution)/shard_map/ppermute | solution.py:85
  65.7 19.2 %collective-permute-start.29 = (bf16[144,768]{1,0:T(8,128)(2,1)S(1)}, bf16[144,768]{1,0:T(8,128)(2,1)S(1)}, u32[]{:S(2)}, u32[]{:S(2)}) collective-permute-start(bf16[144,768]{1,0:T(8,128)(2,1)S(1)} %shard_map.157), channel_id=1, source_target_pairs={{0,2},{1,7},{2,4},{3,1},{4,6},{5,3},{6,0},{7,5},{8,10},{9,15},{10,... | collective-permute-start | bytes 663560 | tf_op jit(solution)/shard_map/ppermute | solution.py:85
  66.0 19.0 %collective-permute-start.30 = (bf16[144,768]{1,0:T(8,128)(2,1)S(1)}, bf16[144,768]{1,0:T(8,128)(2,1)S(1)}, u32[]{:S(2)}, u32[]{:S(2)}) collective-permute-start(bf16[144,768]{1,0:T(8,128)(2,1)S(1)} %shard_map.158), channel_id=1, source_target_pairs={{0,4},{1,5},{2,6},{3,7},{4,0},{5,1},{6,2},{7,3},{8,12},{9,13},{10,... | collective-permute-start | bytes 663560 | tf_op jit(solution)/shard_map/ppermute | solution.py:85
  69.5 15.4 %collective-permute-start.28 = (bf16[144,768]{1,0:T(8,128)(2,1)S(1)}, bf16[144,768]{1,0:T(8,128)(2,1)S(1)}, u32[]{:S(2)}, u32[]{:S(2)}) collective-permute-start(bf16[144,768]{1,0:T(8,128)(2,1)S(1)} %shard_map.156.refs_1_), channel_id=1, source_target_pairs={{0,6},{1,3},{2,0},{3,5},{4,2},{5,7},{6,4},{7,1},{8,14},{9,11},{10,... | collective-permute-start | bytes 663560 | tf_op jit(solution)/shard_map/ppermute | solution.py:85
  79.8 11.9 %collective-permute-start.22 = (bf16[240,768]{1,0:T(8,128)(2,1)S(1)}, bf16[240,768]{1,0:T(8,128)(2,1)S(1)}, u32[]{:S(2)}, u32[]{:S(2)}) collective-permute-start(bf16[240,768]{1,0:T(8,128)(2,1)S(1)} %shard_map.154), channel_id=1, source_target_pairs={{0,2},{1,7},{2,4},{3,1},{4,6},{5,3},{6,0},{7,5},{8,10},{9,15},{10,... | collective-permute-start | bytes 1105928 | tf_op jit(solution)/shard_map/ppermute | solution.py:85
  85.2 10.7 %collective-permute-start.31 = (bf16[48,768]{1,0:T(8,128)(2,1)S(1)}, bf16[48,768]{1,0:T(8,128)(2,1)S(1)}, u32[]{:S(2)}, u32[]{:S(2)}) collective-permute-start(bf16[48,768]{1,0:T(8,128)(2,1)S(1)} %get-tuple-element.44), channel_id=1, source_target_pairs={{0,160},{8,168},{16,176},{24,184},{32,192},{40,200},{48,208},{56,2... | collective-permute-start | bytes 221192 | tf_op jit(solution)/shard_map/ppermute | solution.py:77
  86.9 12.3 %collective-permute-start.32 = (bf16[48,768]{1,0:T(8,128)(2,1)S(1)}, bf16[48,768]{1,0:T(8,128)(2,1)S(1)}, u32[]{:S(2)}, u32[]{:S(2)}) collective-permute-start(bf16[48,768]{1,0:T(8,128)(2,1)S(1)} %get-tuple-element.46), channel_id=1, source_target_pairs={{0,128},{8,136},{16,144},{24,152},{32,160},{40,168},{48,176},{56,1... | collective-permute-start | bytes 221192 | tf_op jit(solution)/shard_map/ppermute | solution.py:77
  89.5 10.0 %collective-permute-start.33 = (bf16[48,768]{1,0:T(8,128)(2,1)S(1)}, bf16[48,768]{1,0:T(8,128)(2,1)S(1)}, u32[]{:S(2)}, u32[]{:S(2)}) collective-permute-start(bf16[48,768]{1,0:T(8,128)(2,1)S(1)} %get-tuple-element.45), channel_id=1, source_target_pairs={{0,96},{8,104},{16,112},{24,120},{32,128},{40,136},{48,144},{56,15... | collective-permute-start | bytes 221192 | tf_op jit(solution)/shard_map/ppermute | solution.py:77
  91.9 7.5 %collective-permute-start.23 = (bf16[48,768]{1,0:T(8,128)(2,1)S(1)}, bf16[48,768]{1,0:T(8,128)(2,1)S(1)}, u32[]{:S(2)}, u32[]{:S(2)}) collective-permute-start(bf16[48,768]{1,0:T(8,128)(2,1)S(1)} %shard_map.155), channel_id=1, source_target_pairs={{0,224},{8,232},{16,240},{24,248},{32,0},{40,8},{48,16},{56,24},{6... | collective-permute-start | bytes 221192 | tf_op jit(solution)/shard_map/ppermute | solution.py:77
  95.7 7.2 %collective-permute-start.24 = (bf16[48,768]{1,0:T(8,128)(2,1)S(1)}, bf16[48,768]{1,0:T(8,128)(2,1)S(1)}, u32[]{:S(2)}, u32[]{:S(2)}) collective-permute-start(bf16[48,768]{1,0:T(8,128)(2,1)S(1)} %get-tuple-element.41), channel_id=1, source_target_pairs={{0,32},{8,40},{16,48},{24,56},{32,64},{40,72},{48,80},{56,88},{64,... | collective-permute-start | bytes 221192 | tf_op jit(solution)/shard_map/ppermute | solution.py:77
  95.8 7.1 %collective-permute-start.25 = (bf16[48,768]{1,0:T(8,128)(2,1)S(1)}, bf16[48,768]{1,0:T(8,128)(2,1)S(1)}, u32[]{:S(2)}, u32[]{:S(2)}) collective-permute-start(bf16[48,768]{1,0:T(8,128)(2,1)S(1)} %get-tuple-element.43), channel_id=1, source_target_pairs={{0,192},{8,200},{16,208},{24,216},{32,224},{40,232},{48,240},{56,2... | collective-permute-start | bytes 221192 | tf_op jit(solution)/shard_map/ppermute | solution.py:77
  99.2 6.5 %collective-permute-start.26 = (bf16[48,768]{1,0:T(8,128)(2,1)S(1)}, bf16[48,768]{1,0:T(8,128)(2,1)S(1)}, u32[]{:S(2)}, u32[]{:S(2)}) collective-permute-start(bf16[48,768]{1,0:T(8,128)(2,1)S(1)} %get-tuple-element.42), channel_id=1, source_target_pairs={{0,64},{8,72},{16,80},{24,88},{32,96},{40,104},{48,112},{56,120},{... | collective-permute-start | bytes 221192 | tf_op jit(solution)/shard_map/ppermute | solution.py:77
  105.9 5.9 %collective-permute-start.34 = (bf16[12,768]{1,0:T(8,128)(2,1)S(1)}, bf16[12,768]{1,0:T(8,128)(2,1)S(1)}, u32[]{:S(2)}, u32[]{:S(2)}) collective-permute-start(bf16[12,768]{1,0:T(8,128)(2,1)S(1)} %get-tuple-element.47), channel_id=1, source_target_pairs={{0,24},{8,0},{16,8},{24,16},{32,56},{40,32},{48,40},{56,48},{64,88... | collective-permute-start | bytes 55304 | tf_op jit(solution)/shard_map/ppermute | solution.py:70
  107.8 5.3 %collective-permute-start.35 = (bf16[12,768]{1,0:T(8,128)(2,1)S(1)}, bf16[12,768]{1,0:T(8,128)(2,1)S(1)}, u32[]{:S(2)}, u32[]{:S(2)}) collective-permute-start(bf16[12,768]{1,0:T(8,128)(2,1)S(1)} %get-tuple-element.49), channel_id=1, source_target_pairs={{0,16},{8,24},{16,0},{24,8},{32,48},{40,56},{48,32},{56,40},{64,80... | collective-permute-start | bytes 55304 | tf_op jit(solution)/shard_map/ppermute | solution.py:70
  109.3 4.1 %collective-permute-start.36 = (bf16[12,768]{1,0:T(8,128)(2,1)S(1)}, bf16[12,768]{1,0:T(8,128)(2,1)S(1)}, u32[]{:S(2)}, u32[]{:S(2)}) collective-permute-start(bf16[12,768]{1,0:T(8,128)(2,1)S(1)} %get-tuple-element.48), channel_id=1, source_target_pairs={{0,8},{8,16},{16,24},{24,0},{32,40},{40,48},{48,56},{56,32},{64,72... | collective-permute-start | bytes 55304 | tf_op jit(solution)/shard_map/ppermute | solution.py:70

commit v2 on v1

--- a/solution.py
+++ b/solution.py
@@ -320,17 +320,17 @@
     send_1, send_2, *keep_a = experts(xs, a, [p2_b])
     got_1, got_2a = swap_core(send_1), swap_core(send_2)
     far_a = join([(a, [(keep_a[0], 0), (got_1, 0)])])
-    behind_a = join([(a, [(keep_a[2], 0), (got_1, a)])])
     relay_a = move_x(far_a, 1)
-    back_a = move_x(behind_a, -1)
 
     xs = [(own_b, 0), (both, a), (p3_b, 0), (p2_b, 0)]
     xs += [(swap_2, a + b), (swap_2, a), (swap_2, a + 2 * b), (swap_3, 0)]
-    send_1, send_2, *keep_b = experts(xs, b, [far_a, behind_a])
+    send_1, send_2, *keep_b = experts(xs, b, [far_a])
     got_1b, got_2b = swap_core(send_1), swap_core(send_2)
+    behind_a = join([(a, [(keep_a[2], 0), (got_1, a)])], [got_1b])
+    back_a = move_x(behind_a, -1)
     last_a = [(keep_a[1], 0), (got_2a, 0), (relay_a, 0)]
     far_b = join([(b, [(keep_b[0], 0), (got_1b, 0)])])
-    both_in = join([(a, last_a)], [back_a, far_b])
+    both_in = join([(a, last_a)], [far_b])
     both = move_x(both_in, 1)
     fore_b = move_x(join([(b, [(keep_b[1], 0), (got_2b, 0)])]), 1)
     back_in = join([(b, [(keep_b[2], 0), (got_1b, b)])])

time: 117 us -> 114 us (0.974)
  waiting for transfers between devices: 45.9 us -> 44.1 us
    ppermute x13, waiting for transfers between devices: 15.2 us -> 13.9 us  [move_z(): return lax.ppermute(value, 'grp', pairs)]
  transfers between devices with their start and end apart: 37 -> 37, of which waited for: 16 -> 18; matrix products, arithmetic and copies ran while one was open for 0% -> 0% of each run, Pallas kernels for 8% -> 8%
where the time goes in v2:
time: 114 us; the launch traced here: 112 us
  starting transfers between devices  52 us (46%)
  waiting for transfers between devices  44.1 us (39%)
  Pallas kernels  13.7 us (12%)
    ppermute x13, starting transfers between devices, move_z(): return lax.ppermute(value, 'grp', pairs)  26.7 us
    ppermute x11, waiting for transfers between devices, move_x(): return lax.ppermute(value, 'tp', pairs)  22.1 us
    ppermute x13, waiting for transfers between devices, move_z(): return lax.ppermute(value, 'grp', pairs)  13.9 us
    ppermute x11, starting transfers between devices, move_x(): return lax.ppermute(value, 'tp', pairs)  13.1 us
    ppermute x6, starting transfers between devices, move_y(): return lax.ppermute(value, 'grp', pairs)  10.8 us
    pallas_call x1, Pallas kernels, attend(): pl.pallas_call(lambda *refs: attend_kernel(*refs[:6], *refs[6 + len(after...  6.41 us
    pallas_call x2, Pallas kernels, mlp(): pl.pallas_call(functools.partial(mlp_kernel, tuple(starts), rows), out_sh...  5.37 us
    ppermute x6, waiting for transfers between devices, move_y(): return lax.ppermute(value, 'grp', pairs)  4.92 us
  transfers between devices with their start and end apart: 37, of which 18 were waited for; matrix products, arithmetic and copies ran while one was open for 0% of the time, Pallas kernels for 8%

profile of v2, /device:TPU:8, one launch (start us, length us, event | category | flops | bytes accessed | tf_op | source)
XLA Modules:
  0.0 112.3 jit_solution(1062696846605168633)
XLA Ops:
  0.6 1.2 %shard_map.140 = (f32[48,16]{1,0:T(8,128)S(1)}, bf16[12,768]{1,0:T(8,128)(2,1)S(1)}, bf16[12,768]{1,0:T(8,128)(2,1)S(1)}, bf16[12,768]{1,0:T(8,128)(2,1)S(1)}, bf16[12,768]{1,0:T(8,128)(2,1)S(1)}) custom-call(s32[1]{0:T(128)} %bitcast.grp, s32[1]{0:T(128)} %bitcast.1.tp, s32[2,16]{1,0:T(2,128)} %bitcast.18, f32[2,16]{1,0:T(2,128)} %bitcast.19, ...), custom_call_target="tpu_custom_call" | custom-call | tf_op jit(solution)/shard_map/pallas_call | solution.py:133
  1.9 1.7 %collective-permute-start = (bf16[12,768]{1,0:T(8,128)(2,1)S(1)}, bf16[12,768]{1,0:T(8,128)(2,1)S(1)}, u32[]{:S(2)}, u32[]{:S(2)}) collective-permute-start(bf16[12,768]{1,0:T(8,128)(2,1)S(1)} %get-tuple-element.20), channel_id=1, source_target_pairs={{0,8},{8,16},{16,24},{24,0},{32,40},{40,48},{48,56},{56,32},{64,72... | collective-permute-start | bytes 55304 | tf_op jit(solution)/shard_map/ppermute | solution.py:70
  3.5 2.7 %collective-permute-start.1 = (bf16[12,768]{1,0:T(8,128)(2,1)S(1)}, bf16[12,768]{1,0:T(8,128)(2,1)S(1)}, u32[]{:S(2)}, u32[]{:S(2)}) collective-permute-start(bf16[12,768]{1,0:T(8,128)(2,1)S(1)} %get-tuple-element.21), channel_id=1, source_target_pairs={{0,16},{8,24},{16,0},{24,8},{32,48},{40,56},{48,32},{56,40},{64,80... | collective-permute-start | bytes 55304 | tf_op jit(solution)/shard_map/ppermute | solution.py:70
  6.2 0.7 collective-permute-start.2
  6.9 2.0 %collective-permute-done.1 = bf16[12,768]{1,0:T(8,128)(2,1)S(1)} collective-permute-done((bf16[12,768]{1,0:T(8,128)(2,1)S(1)}, bf16[12,768]{1,0:T(8,128)(2,1)S(1)}, u32[]{:S(2)}, u32[]{:S(2)}) %collective-permute-start.1) | collective-permute-done | bytes 18464 | tf_op jit(solution)/shard_map/ppermute | solution.py:70
  8.9 1.2 %collective-permute-done.2 = bf16[12,768]{1,0:T(8,128)(2,1)S(1)} collective-permute-done((bf16[12,768]{1,0:T(8,128)(2,1)S(1)}, bf16[12,768]{1,0:T(8,128)(2,1)S(1)}, u32[]{:S(2)}, u32[]{:S(2)}) %collective-permute-start.2) | collective-permute-done | bytes 18464 | tf_op jit(solution)/shard_map/ppermute | solution.py:70
  10.1 5.2 %collective-permute-start.6 = (bf16[48,768]{1,0:T(8,128)(2,1)S(1)}, bf16[48,768]{1,0:T(8,128)(2,1)S(1)}, u32[]{:S(2)}, u32[]{:S(2)}) collective-permute-start(bf16[48,768]{1,0:T(8,128)(2,1)S(1)} %pad_maximum_fusion.refs_0_), channel_id=1, source_target_pairs={{0,192},{8,200},{16,208},{24,216},{32,224},{40,232},{48,240},{56,2... | collective-permute-start | bytes 221192 | tf_op jit(solution)/shard_map/ppermute | solution.py:77
  15.3 3.7 %collective-permute-start.4 = (bf16[48,768]{1,0:T(8,128)(2,1)S(1)}, bf16[48,768]{1,0:T(8,128)(2,1)S(1)}, u32[]{:S(2)}, u32[]{:S(2)}) collective-permute-start(bf16[48,768]{1,0:T(8,128)(2,1)S(1)} %pad_maximum_fusion.refs_0_), channel_id=1, source_target_pairs={{0,224},{8,232},{16,240},{24,248},{32,0},{40,8},{48,16},{56,24},{6... | collective-permute-start | bytes 221192 | tf_op jit(solution)/shard_map/ppermute | solution.py:77
  19.0 3.0 %collective-permute-done.5.refs_3_.refs_1_ = bf16[48,768]{1,0:T(8,128)(2,1)S(1)} collective-permute-done((bf16[48,768]{1,0:T(8,128)(2,1)S(1)}, bf16[48,768]{1,0:T(8,128)(2,1)S(1)}, u32[]{:S(2)}, u32[]{:S(2)}) %collective-permute-start.5) | collective-permute-done | bytes 73760 | tf_op jit(solution)/shard_map/ppermute | solution.py:77
  22.0 2.5 %collective-permute-done.3.refs_1_.refs_0_ = bf16[48,768]{1,0:T(8,128)(2,1)S(1)} collective-permute-done((bf16[48,768]{1,0:T(8,128)(2,1)S(1)}, bf16[48,768]{1,0:T(8,128)(2,1)S(1)}, u32[]{:S(2)}, u32[]{:S(2)}) %collective-permute-start.3) | collective-permute-done | bytes 73760 | tf_op jit(solution)/shard_map/ppermute | solution.py:77
  24.6 2.8 %collective-permute-start.10 = (bf16[240,768]{1,0:T(8,128)(2,1)S(1)}, bf16[240,768]{1,0:T(8,128)(2,1)S(1)}, u32[]{:S(2)}, u32[]{:S(2)}) collective-permute-start(bf16[240,768]{1,0:T(8,128)(2,1)S(1)} %shard_map.141.refs_0_), channel_id=1, source_target_pairs={{0,6},{1,3},{2,0},{3,5},{4,2},{5,7},{6,4},{7,1},{8,14},{9,11},{10,... | collective-permute-start | bytes 1105928 | tf_op jit(solution)/shard_map/ppermute | solution.py:85
  27.4 0.1 collective-permute-start.8
  27.5 4.1 %collective-permute-start.9 = (bf16[48,768]{1,0:T(8,128)(2,1)S(1)}, bf16[48,768]{1,0:T(8,128)(2,1)S(1)}, u32[]{:S(2)}, u32[]{:S(2)}) collective-permute-start(bf16[48,768]{1,0:T(8,128)(2,1)S(1)} %collective-permute-done.4.refs_2_), channel_id=1, source_target_pairs={{0,192},{8,200},{16,208},{24,216},{32,224},{40,232},{48,240},{56,2... | collective-permute-start | bytes 221192 | tf_op jit(solution)/shard_map/ppermute | solution.py:77
  31.6 2.4 %collective-permute-done.9.refs_1_ = bf16[48,768]{1,0:T(8,128)(2,1)S(1)} collective-permute-done((bf16[48,768]{1,0:T(8,128)(2,1)S(1)}, bf16[48,768]{1,0:T(8,128)(2,1)S(1)}, u32[]{:S(2)}, u32[]{:S(2)}) %collective-permute-start.9) | collective-permute-done | bytes 73760 | tf_op jit(solution)/shard_map/ppermute | solution.py:77
  34.1 1.4 %collective-permute-done.8.refs_0_ = bf16[96,768]{1,0:T(8,128)(2,1)S(1)} collective-permute-done((bf16[96,768]{1,0:T(8,128)(2,1)S(1)}, bf16[96,768]{1,0:T(8,128)(2,1)S(1)}, u32[]{:S(2)}, u32[]{:S(2)}) %collective-permute-start.8) | collective-permute-done | bytes 147488 | tf_op jit(solution)/shard_map/ppermute | solution.py:77
  35.6 0.5 collective-permute-done.7.refs_0_.refs_1_
  36.2 0.2 collective-permute-start.11
  36.4 3.1 %collective-permute-start.13 = (bf16[144,768]{1,0:T(8,128)(2,1)S(1)}, bf16[144,768]{1,0:T(8,128)(2,1)S(1)}, u32[]{:S(2)}, u32[]{:S(2)}) collective-permute-start(bf16[144,768]{1,0:T(8,128)(2,1)S(1)} %shard_map.143.refs_1_.refs_7_.refs_0_), channel_id=1, source_target_pairs={{0,6},{1,3},{2,0},{3,5},{4,2},{5,7},{6,4},{7,1},{8,14},{9,11},{10,... | collective-permute-start | bytes 663560 | tf_op jit(solution)/shard_map/ppermute | solution.py:85
  39.5 0.1 shard_map.146
  39.6 0.1 collective-permute-start.12
  39.7 6.4 %shard_map.145.refs_3_ = bf16[16,768]{1,0:T(8,128)(2,1)} custom-call(s32[16]{0:T(128)S(1)} %copy-done.9, bf16[16,768]{1,0:T(8,128)(2,1)S(1)} %copy-done.6, bf16[16,128]{1,0:T(8,128)(2,1)S(1)} %copy-done.7, bf16[16,128]{1,0:T(8,128)(2,1)S(1)} %copy-done.8, bf16[16,256,128]{2,1,0:T(8,128)(2,1)S(1)} %copy-done.3, bf16[16,256,128]{2,1,0:T(8,128)(2,1)S(1)} %copy-done.4, ...), custom_call_target="tpu_custom_call" | custom-call | tf_op jit(solution)/shard_map/pallas_call | solution.py:56
  46.2 1.2 %collective-permute-done.11.refs_0_.refs_3_.refs_1_ = bf16[384,768]{1,0:T(8,128)(2,1)S(1)} collective-permute-done((bf16[384,768]{1,0:T(8,128)(2,1)S(1)}, bf16[384,768]{1,0:T(8,128)(2,1)S(1)}, u32[]{:S(2)}, u32[]{:S(2)}) %collective-permute-start.11) | collective-permute-done | bytes 589856 | tf_op jit(solution)/shard_map/ppermute | solution.py:85
  47.3 0.1 shard_map.148
  47.4 0.1 collective-permute-start.14
  47.5 0.3 collective-permute-start.15
  47.8 7.1 %collective-permute-done.15.refs_10_.refs_3_ = bf16[144,768]{1,0:T(8,128)(2,1)S(1)} collective-permute-done((bf16[144,768]{1,0:T(8,128)(2,1)S(1)}, bf16[144,768]{1,0:T(8,128)(2,1)S(1)}, u32[]{:S(2)}, u32[]{:S(2)}) %collective-permute-start.15) | collective-permute-done | bytes 221216 | tf_op jit(solution)/shard_map/ppermute | solution.py:85
  55.0 3.2 %shard_map.149 = (bf16[480,768]{1,0:T(8,128)(2,1)S(1)}, bf16[480,768]{1,0:T(8,128)(2,1)S(1)}, f32[240,768]{1,0:T(8,128)S(1)}, f32[240,768]{1,0:T(8,128)S(1)}, f3...) custom-call(s32[1]{0:T(128)} %bitcast.1.tp, bf16[240,768]{1,0:T(8,128)(2,1)S(1)} %shard_map.141.refs_0_, ...), custom_call_target="tpu_custom_call" | custom-call | tf_op jit(solution)/shard_map/pallas_call | solution.py:217
  58.2 0.1 collective-permute-start.17
  58.3 0.5 collective-permute-start.18
  58.7 0.1 collective-permute-start.16
  58.8 1.6 %collective-permute-done.17.refs_1_ = bf16[480,768]{1,0:T(8,128)(2,1)S(1)} collective-permute-done((bf16[480,768]{1,0:T(8,128)(2,1)S(1)}, bf16[480,768]{1,0:T(8,128)(2,1)S(1)}, u32[]{:S(2)}, u32[]{:S(2)}) %collective-permute-start.17) | collective-permute-done | bytes 737312 | tf_op jit(solution)/shard_map/ppermute | solution.py:89
  60.5 0.1 shard_map.150.refs_10_
  60.5 0.2 collective-permute-done.18.refs_5_
  60.8 2.2 %shard_map.151 = (bf16[288,768]{1,0:T(8,128)(2,1)S(1)}, bf16[288,768]{1,0:T(8,128)(2,1)S(1)}, f32[144,768]{1,0:T(8,128)S(1)}, f32[144,768]{1,0:T(8,128)S(1)}, f3...) custom-call(s32[1]{0:T(128)} %bitcast.1.tp, bf16[144,768]{1,0:T(8,128)(2,1)S(1)} %shard_map.143.refs_1_.refs_7_.refs_0_, ...), custom_call_target="tpu_custom_call" | custom-call | tf_op jit(solution)/shard_map/pallas_call | solution.py:217
  63.0 0.2 collective-permute-start.19
  63.2 0.4 collective-permute-start.27
  63.6 1.3 %collective-permute-done.19.refs_2_.refs_1_ = bf16[288,768]{1,0:T(8,128)(2,1)S(1)} collective-permute-done((bf16[288,768]{1,0:T(8,128)(2,1)S(1)}, bf16[288,768]{1,0:T(8,128)(2,1)S(1)}, u32[]{:S(2)}, u32[]{:S(2)}) %collective-permute-start.19) | collective-permute-done | bytes 442400 | tf_op jit(solution)/shard_map/ppermute | solution.py:89
  64.9 2.0 %collective-permute-start.28 = (bf16[144,768]{1,0:T(8,128)(2,1)S(1)}, bf16[144,768]{1,0:T(8,128)(2,1)S(1)}, u32[]{:S(2)}, u32[]{:S(2)}) collective-permute-start(bf16[144,768]{1,0:T(8,128)(2,1)S(1)} %shard_map.156.refs_1_), channel_id=1, source_target_pairs={{0,6},{1,3},{2,0},{3,5},{4,2},{5,7},{6,4},{7,1},{8,14},{9,11},{10,... | collective-permute-start | bytes 663560 | tf_op jit(solution)/shard_map/ppermute | solution.py:85
  67.0 0.1 collective-permute-start.30
  67.2 0.9 collective-permute-start.29
  68.1 12.3 %collective-permute-done.21.refs_2_ = bf16[240,768]{1,0:T(8,128)(2,1)S(1)} collective-permute-done((bf16[240,768]{1,0:T(8,128)(2,1)S(1)}, bf16[240,768]{1,0:T(8,128)(2,1)S(1)}, u32[]{:S(2)}, u32[]{:S(2)}) %collective-permute-start.21) | collective-permute-done | bytes 368672 | tf_op jit(solution)/shard_map/ppermute | solution.py:85
  80.4 0.2 shard_map.154
  80.6 0.1 collective-permute-start.22
  80.7 0.1 shard_map.152
  80.8 3.5 %collective-permute-start.20 = (bf16[240,768]{1,0:T(8,128)(2,1)S(1)}, bf16[240,768]{1,0:T(8,128)(2,1)S(1)}, u32[]{:S(2)}, u32[]{:S(2)}) collective-permute-start(bf16[240,768]{1,0:T(8,128)(2,1)S(1)} %shard_map.152), channel_id=1, source_target_pairs={{0,6},{1,3},{2,0},{3,5},{4,2},{5,7},{6,4},{7,1},{8,14},{9,11},{10,... | collective-permute-start | bytes 1105928 | tf_op jit(solution)/shard_map/ppermute | solution.py:85
  84.3 0.9 collective-permute-done.29
  85.2 0.2 add_convert_fusion
  85.4 0.4 collective-permute-start.31
  85.8 3.5 %collective-permute-start.33 = (bf16[48,768]{1,0:T(8,128)(2,1)S(1)}, bf16[48,768]{1,0:T(8,128)(2,1)S(1)}, u32[]{:S(2)}, u32[]{:S(2)}) collective-permute-start(bf16[48,768]{1,0:T(8,128)(2,1)S(1)} %get-tuple-element.45), channel_id=1, source_target_pairs={{0,96},{8,104},{16,112},{24,120},{32,128},{40,136},{48,144},{56,15... | collective-permute-start | bytes 221192 | tf_op jit(solution)/shard_map/ppermute | solution.py:77
  89.3 1.4 %collective-permute-start.32 = (bf16[48,768]{1,0:T(8,128)(2,1)S(1)}, bf16[48,768]{1,0:T(8,128)(2,1)S(1)}, u32[]{:S(2)}, u32[]{:S(2)}) collective-permute-start(bf16[48,768]{1,0:T(8,128)(2,1)S(1)} %get-tuple-element.46), channel_id=1, source_target_pairs={{0,128},{8,136},{16,144},{24,152},{32,160},{40,168},{48,176},{56,1... | collective-permute-start | bytes 221192 | tf_op jit(solution)/shard_map/ppermute | solution.py:77
  90.7 0.2 fusion.16
  91.0 1.6 %collective-permute-start.24 = (bf16[48,768]{1,0:T(8,128)(2,1)S(1)}, bf16[48,768]{1,0:T(8,128)(2,1)S(1)}, u32[]{:S(2)}, u32[]{:S(2)}) collective-permute-start(bf16[48,768]{1,0:T(8,128)(2,1)S(1)} %get-tuple-element.41), channel_id=1, source_target_pairs={{0,32},{8,40},{16,48},{24,56},{32,64},{40,72},{48,80},{56,88},{64,... | collective-permute-start | bytes 221192 | tf_op jit(solution)/shard_map/ppermute | solution.py:77
  92.6 3.3 %collective-permute-start.26 = (bf16[48,768]{1,0:T(8,128)(2,1)S(1)}, bf16[48,768]{1,0:T(8,128)(2,1)S(1)}, u32[]{:S(2)}, u32[]{:S(2)}) collective-permute-start(bf16[48,768]{1,0:T(8,128)(2,1)S(1)} %get-tuple-element.42), channel_id=1, source_target_pairs={{0,64},{8,72},{16,80},{24,88},{32,96},{40,104},{48,112},{56,120},{... | collective-permute-start | bytes 221192 | tf_op jit(solution)/shard_map/ppermute | solution.py:77
  95.9 1.1 collective-permute-start.25
  97.0 2.3 %collective-permute-start.23 = (bf16[48,768]{1,0:T(8,128)(2,1)S(1)}, bf16[48,768]{1,0:T(8,128)(2,1)S(1)}, u32[]{:S(2)}, u32[]{:S(2)}) collective-permute-start(bf16[48,768]{1,0:T(8,128)(2,1)S(1)} %shard_map.155), channel_id=1, source_target_pairs={{0,224},{8,232},{16,240},{24,248},{32,0},{40,8},{48,16},{56,24},{6... | collective-permute-start | bytes 221192 | tf_op jit(solution)/shard_map/ppermute | solution.py:77
  99.3 1.5 %collective-permute-done.26 = bf16[48,768]{1,0:T(8,128)(2,1)S(1)} collective-permute-done((bf16[48,768]{1,0:T(8,128)(2,1)S(1)}, bf16[48,768]{1,0:T(8,128)(2,1)S(1)}, u32[]{:S(2)}, u32[]{:S(2)}) %collective-permute-start.26) | collective-permute-done | bytes 73760 | tf_op jit(solution)/shard_map/ppermute | solution.py:77
  100.8 1.3 %collective-permute-done.25 = bf16[48,768]{1,0:T(8,128)(2,1)S(1)} collective-permute-done((bf16[48,768]{1,0:T(8,128)(2,1)S(1)}, bf16[48,768]{1,0:T(8,128)(2,1)S(1)}, u32[]{:S(2)}, u32[]{:S(2)}) %collective-permute-start.25) | collective-permute-done | bytes 73760 | tf_op jit(solution)/shard_map/ppermute | solution.py:77
  102.0 1.7 %collective-permute-done.23 = bf16[48,768]{1,0:T(8,128)(2,1)S(1)} collective-permute-done((bf16[48,768]{1,0:T(8,128)(2,1)S(1)}, bf16[48,768]{1,0:T(8,128)(2,1)S(1)}, u32[]{:S(2)}, u32[]{:S(2)}) %collective-permute-start.23) | collective-permute-done | bytes 73760 | tf_op jit(solution)/shard_map/ppermute | solution.py:77
  103.7 0.1 fusion.14
  103.8 2.0 %collective-permute-start.34 = (bf16[12,768]{1,0:T(8,128)(2,1)S(1)}, bf16[12,768]{1,0:T(8,128)(2,1)S(1)}, u32[]{:S(2)}, u32[]{:S(2)}) collective-permute-start(bf16[12,768]{1,0:T(8,128)(2,1)S(1)} %get-tuple-element.47), channel_id=1, source_target_pairs={{0,24},{8,0},{16,8},{24,16},{32,56},{40,32},{48,40},{56,48},{64,88... | collective-permute-start | bytes 55304 | tf_op jit(solution)/shard_map/ppermute | solution.py:70
  105.8 0.1 collective-permute-start.36
  105.9 3.7 %collective-permute-start.35 = (bf16[12,768]{1,0:T(8,128)(2,1)S(1)}, bf16[12,768]{1,0:T(8,128)(2,1)S(1)}, u32[]{:S(2)}, u32[]{:S(2)}) collective-permute-start(bf16[12,768]{1,0:T(8,128)(2,1)S(1)} %get-tuple-element.49), channel_id=1, source_target_pairs={{0,16},{8,24},{16,0},{24,8},{32,48},{40,56},{48,32},{56,40},{64,80... | collective-permute-start | bytes 55304 | tf_op jit(solution)/shard_map/ppermute | solution.py:70
  109.7 1.8 %collective-permute-done.35 = bf16[12,768]{1,0:T(8,128)(2,1)S(1)} collective-permute-done((bf16[12,768]{1,0:T(8,128)(2,1)S(1)}, bf16[12,768]{1,0:T(8,128)(2,1)S(1)}, u32[]{:S(2)}, u32[]{:S(2)}) %collective-permute-start.35) | collective-permute-done | bytes 18464 | tf_op jit(solution)/shard_map/ppermute | solution.py:70
  111.4 0.9 convolution_convert_fusion
  (61 shorter events, 0.5 us)
Async XLA Ops:
  0.6 38.8 %copy-start = (bf16[1,256,6144]{2,1,0:T(8,128)(2,1)S(1)}, bf16[1,256,6144]{2,1,0:T(8,128)(2,1)}, u32[]{:S(2)}) copy-start(bf16[1,256,6144]{2,1,0:T(8,128)(2,1)} %param.25) | copy-start | bytes 9437188
  1.9 5.0 %collective-permute-start = (bf16[12,768]{1,0:T(8,128)(2,1)S(1)}, bf16[12,768]{1,0:T(8,128)(2,1)S(1)}, u32[]{:S(2)}, u32[]{:S(2)}) collective-permute-start(bf16[12,768]{1,0:T(8,128)(2,1)S(1)} %get-tuple-element.20), channel_id=1, source_target_pairs={{0,8},{8,16},{16,24},{24,0},{32,40},{40,48},{48,56},{56,32},{64,72... | collective-permute-start | bytes 55304 | tf_op jit(solution)/shard_map/ppermute | solution.py:70
  3.5 5.3 %collective-permute-start.1 = (bf16[12,768]{1,0:T(8,128)(2,1)S(1)}, bf16[12,768]{1,0:T(8,128)(2,1)S(1)}, u32[]{:S(2)}, u32[]{:S(2)}) collective-permute-start(bf16[12,768]{1,0:T(8,128)(2,1)S(1)} %get-tuple-element.21), channel_id=1, source_target_pairs={{0,16},{8,24},{16,0},{24,8},{32,48},{40,56},{48,32},{56,40},{64,80... | collective-permute-start | bytes 55304 | tf_op jit(solution)/shard_map/ppermute | solution.py:70
  6.2 3.8 %collective-permute-start.2 = (bf16[12,768]{1,0:T(8,128)(2,1)S(1)}, bf16[12,768]{1,0:T(8,128)(2,1)S(1)}, u32[]{:S(2)}, u32[]{:S(2)}) collective-permute-start(bf16[12,768]{1,0:T(8,128)(2,1)S(1)} %get-tuple-element.22), channel_id=1, source_target_pairs={{0,24},{8,0},{16,8},{24,16},{32,56},{40,32},{48,40},{56,48},{64,88... | collective-permute-start | bytes 55304 | tf_op jit(solution)/shard_map/ppermute | solution.py:70
  10.1 8.9 %collective-permute-start.6 = (bf16[48,768]{1,0:T(8,128)(2,1)S(1)}, bf16[48,768]{1,0:T(8,128)(2,1)S(1)}, u32[]{:S(2)}, u32[]{:S(2)}) collective-permute-start(bf16[48,768]{1,0:T(8,128)(2,1)S(1)} %pad_maximum_fusion.refs_0_), channel_id=1, source_target_pairs={{0,192},{8,200},{16,208},{24,216},{32,224},{40,232},{48,240},{56,2... | collective-permute-start | bytes 221192 | tf_op jit(solution)/shard_map/ppermute | solution.py:77
  15.3 6.7 %collective-permute-start.5 = (bf16[48,768]{1,0:T(8,128)(2,1)S(1)}, bf16[48,768]{1,0:T(8,128)(2,1)S(1)}, u32[]{:S(2)}, u32[]{:S(2)}) collective-permute-start(bf16[48,768]{1,0:T(8,128)(2,1)S(1)} %pad_maximum_fusion.refs_0_), channel_id=1, source_target_pairs={{0,64},{8,72},{16,80},{24,88},{32,96},{40,104},{48,112},{56,120},{... | collective-permute-start | bytes 221192 | tf_op jit(solution)/shard_map/ppermute | solution.py:77
  15.3 6.7 %collective-permute-start.4 = (bf16[48,768]{1,0:T(8,128)(2,1)S(1)}, bf16[48,768]{1,0:T(8,128)(2,1)S(1)}, u32[]{:S(2)}, u32[]{:S(2)}) collective-permute-start(bf16[48,768]{1,0:T(8,128)(2,1)S(1)} %pad_maximum_fusion.refs_0_), channel_id=1, source_target_pairs={{0,224},{8,232},{16,240},{24,248},{32,0},{40,8},{48,16},{56,24},{6... | collective-permute-start | bytes 221192 | tf_op jit(solution)/shard_map/ppermute | solution.py:77
  19.0 5.6 %collective-permute-start.3 = (bf16[48,768]{1,0:T(8,128)(2,1)S(1)}, bf16[48,768]{1,0:T(8,128)(2,1)S(1)}, u32[]{:S(2)}, u32[]{:S(2)}) collective-permute-start(bf16[48,768]{1,0:T(8,128)(2,1)S(1)} %pad_maximum_fusion.refs_0_), channel_id=1, source_target_pairs={{0,32},{8,40},{16,48},{24,56},{32,64},{40,72},{48,80},{56,88},{64,... | collective-permute-start | bytes 221192 | tf_op jit(solution)/shard_map/ppermute | solution.py:77
  24.6 11.0 %collective-permute-start.10 = (bf16[240,768]{1,0:T(8,128)(2,1)S(1)}, bf16[240,768]{1,0:T(8,128)(2,1)S(1)}, u32[]{:S(2)}, u32[]{:S(2)}) collective-permute-start(bf16[240,768]{1,0:T(8,128)(2,1)S(1)} %shard_map.141.refs_0_), channel_id=1, source_target_pairs={{0,6},{1,3},{2,0},{3,5},{4,2},{5,7},{6,4},{7,1},{8,14},{9,11},{10,... | collective-permute-start | bytes 1105928 | tf_op jit(solution)/shard_map/ppermute | solution.py:85
  27.4 8.7 %collective-permute-start.7 = (bf16[240,768]{1,0:T(8,128)(2,1)S(1)}, bf16[240,768]{1,0:T(8,128)(2,1)S(1)}, u32[]{:S(2)}, u32[]{:S(2)}) collective-permute-start(bf16[240,768]{1,0:T(8,128)(2,1)S(1)} %shard_map.141.refs_0_), channel_id=1, source_target_pairs={{0,2},{1,7},{2,4},{3,1},{4,6},{5,3},{6,0},{7,5},{8,10},{9,15},{10,... | collective-permute-start | bytes 1105928 | tf_op jit(solution)/shard_map/ppermute | solution.py:85
  27.4 8.1 %collective-permute-start.8 = (bf16[96,768]{1,0:T(8,128)(2,1)S(1)}, bf16[96,768]{1,0:T(8,128)(2,1)S(1)}, u32[]{:S(2)}, u32[]{:S(2)}) collective-permute-start(bf16[96,768]{1,0:T(8,128)(2,1)S(1)} %shard_map.142), channel_id=1, source_target_pairs={{0,64},{8,72},{16,80},{24,88},{32,96},{40,104},{48,112},{56,120},{... | collective-permute-start | bytes 442376 | tf_op jit(solution)/shard_map/ppermute | solution.py:77
  27.5 6.6 %collective-permute-start.9 = (bf16[48,768]{1,0:T(8,128)(2,1)S(1)}, bf16[48,768]{1,0:T(8,128)(2,1)S(1)}, u32[]{:S(2)}, u32[]{:S(2)}) collective-permute-start(bf16[48,768]{1,0:T(8,128)(2,1)S(1)} %collective-permute-done.4.refs_2_), channel_id=1, source_target_pairs={{0,192},{8,200},{16,208},{24,216},{32,224},{40,232},{48,240},{56,2... | collective-permute-start | bytes 221192 | tf_op jit(solution)/shard_map/ppermute | solution.py:77
  35.5 4.2 %copy-start.3 = (bf16[16,256,128]{2,1,0:T(8,128)(2,1)S(1)}, bf16[16,256,128]{2,1,0:T(8,128)(2,1)}, u32[]{:S(2)}) copy-start(bf16[16,256,128]{2,1,0:T(8,128)(2,1)} %refs_4_.1) | copy-start | bytes 3145732
  35.5 4.2 %copy-start.4 = (bf16[16,256,128]{2,1,0:T(8,128)(2,1)S(1)}, bf16[16,256,128]{2,1,0:T(8,128)(2,1)}, u32[]{:S(2)}) copy-start(bf16[16,256,128]{2,1,0:T(8,128)(2,1)} %refs_5_.1) | copy-start | bytes 3145732
  35.5 4.2 %copy-start.6 = (bf16[16,768]{1,0:T(8,128)(2,1)S(1)}, bf16[16,768]{1,0:T(8,128)(2,1)}, u32[]{:S(2)}) copy-start(bf16[16,768]{1,0:T(8,128)(2,1)} %refs_1_.1) | copy-start | bytes 73732
  35.5 4.2 %copy-start.7 = (bf16[16,128]{1,0:T(8,128)(2,1)S(1)}, bf16[16,128]{1,0:T(8,128)(2,1)}, u32[]{:S(2)}) copy-start(bf16[16,128]{1,0:T(8,128)(2,1)} %refs_2_.1) | copy-start | bytes 12292
  35.5 4.2 %copy-start.8 = (bf16[16,128]{1,0:T(8,128)(2,1)S(1)}, bf16[16,128]{1,0:T(8,128)(2,1)}, u32[]{:S(2)}) copy-start(bf16[16,128]{1,0:T(8,128)(2,1)} %refs_3_.1) | copy-start | bytes 12292
  35.6 4.2 %copy-start.9 = (s32[16]{0:T(128)S(1)}, s32[16]{0:T(128)}, u32[]{:S(2)}) copy-start(s32[16]{0:T(128)} %refs_0_.1) | copy-start | bytes 196
  36.2 11.2 %collective-permute-start.11 = (bf16[384,768]{1,0:T(8,128)(2,1)S(1)}, bf16[384,768]{1,0:T(8,128)(2,1)S(1)}, u32[]{:S(2)}, u32[]{:S(2)}) collective-permute-start(bf16[384,768]{1,0:T(8,128)(2,1)S(1)} %shard_map.144.refs_6_), channel_id=1, source_target_pairs={{0,2},{1,7},{2,4},{3,1},{4,6},{5,3},{6,0},{7,5},{8,10},{9,15},{10,... | collective-permute-start | bytes 1769480 | tf_op jit(solution)/shard_map/ppermute | solution.py:85
  36.4 9.8 %collective-permute-start.13 = (bf16[144,768]{1,0:T(8,128)(2,1)S(1)}, bf16[144,768]{1,0:T(8,128)(2,1)S(1)}, u32[]{:S(2)}, u32[]{:S(2)}) collective-permute-start(bf16[144,768]{1,0:T(8,128)(2,1)S(1)} %shard_map.143.refs_1_.refs_7_.refs_0_), channel_id=1, source_target_pairs={{0,6},{1,3},{2,0},{3,5},{4,2},{5,7},{6,4},{7,1},{8,14},{9,11},{10,... | collective-permute-start | bytes 663560 | tf_op jit(solution)/shard_map/ppermute | solution.py:85
  39.5 15.5 %copy-start.5 = (f32[6144]{0:T(1024)S(1)}, f32[6144]{0:T(1024)}, u32[]{:S(2)}) copy-start(f32[6144]{0:T(1024)} %param.20) | copy-start | bytes 73732
  39.6 15.4 %copy-start.1 = (bf16[1,6144,256]{2,1,0:T(8,128)(2,1)S(1)}, bf16[1,6144,256]{2,1,0:T(8,128)(2,1)}, u32[]{:S(2)}) copy-start(bf16[1,6144,256]{2,1,0:T(8,128)(2,1)} %param.23) | copy-start | bytes 9437188
  39.6 15.4 %copy-start.2 = (bf16[1,6144,256]{2,1,0:T(8,128)(2,1)S(1)}, bf16[1,6144,256]{2,1,0:T(8,128)(2,1)}, u32[]{:S(2)}) copy-start(bf16[1,6144,256]{2,1,0:T(8,128)(2,1)} %param.24) | copy-start | bytes 9437188
  39.6 15.4 %collective-permute-start.12 = (bf16[720,768]{1,0:T(8,128)(2,1)S(1)}, bf16[720,768]{1,0:T(8,128)(2,1)S(1)}, u32[]{:S(2)}, u32[]{:S(2)}) collective-permute-start(bf16[720,768]{1,0:T(8,128)(2,1)S(1)} %shard_map.146), channel_id=1, source_target_pairs={{0,1},{1,0},{2,3},{3,2},{4,5},{5,4},{6,7},{7,6},{8,9},{9,8},{10,11... | collective-permute-start | bytes 3317768 | tf_op jit(solution)/shard_map/ppermute | solution.py:89
  47.4 7.5 %collective-permute-start.14 = (bf16[672,768]{1,0:T(8,128)(2,1)S(1)}, bf16[672,768]{1,0:T(8,128)(2,1)S(1)}, u32[]{:S(2)}, u32[]{:S(2)}) collective-permute-start(bf16[672,768]{1,0:T(8,128)(2,1)S(1)} %shard_map.148), channel_id=1, source_target_pairs={{0,1},{1,0},{2,3},{3,2},{4,5},{5,4},{6,7},{7,6},{8,9},{9,8},{10,11... | collective-permute-start | bytes 3096584 | tf_op jit(solution)/shard_map/ppermute | solution.py:89
  47.5 7.4 %collective-permute-start.15 = (bf16[144,768]{1,0:T(8,128)(2,1)S(1)}, bf16[144,768]{1,0:T(8,128)(2,1)S(1)}, u32[]{:S(2)}, u32[]{:S(2)}) collective-permute-start(bf16[144,768]{1,0:T(8,128)(2,1)S(1)} %shard_map.147.refs_4_), channel_id=1, source_target_pairs={{0,2},{1,7},{2,4},{3,1},{4,6},{5,3},{6,0},{7,5},{8,10},{9,15},{10,... | collective-permute-start | bytes 663560 | tf_op jit(solution)/shard_map/ppermute | solution.py:85
  58.2 2.3 %collective-permute-start.17 = (bf16[480,768]{1,0:T(8,128)(2,1)S(1)}, bf16[480,768]{1,0:T(8,128)(2,1)S(1)}, u32[]{:S(2)}, u32[]{:S(2)}) collective-permute-start(bf16[480,768]{1,0:T(8,128)(2,1)S(1)} %get-tuple-element.27), channel_id=1, source_target_pairs={{0,1},{1,0},{2,3},{3,2},{4,5},{5,4},{6,7},{7,6},{8,9},{9,8},{10,11... | collective-permute-start | bytes 2211848 | tf_op jit(solution)/shard_map/ppermute | solution.py:89
  58.3 2.5 %collective-permute-start.18 = (bf16[144,768]{1,0:T(8,128)(2,1)S(1)}, bf16[144,768]{1,0:T(8,128)(2,1)S(1)}, u32[]{:S(2)}, u32[]{:S(2)}) collective-permute-start(bf16[144,768]{1,0:T(8,128)(2,1)S(1)} %collective-permute-done.15.refs_10_.refs_3_), channel_id=1, source_target_pairs={{0,1},{1,0},{2,3},{3,2},{4,5},{5,4},{6,7},{7,6},{8,9},{9,8},{10,11... | collective-permute-start | bytes 663560 | tf_op jit(solution)/shard_map/ppermute | solution.py:89
  58.7 9.4 %collective-permute-start.16 = (bf16[480,768]{1,0:T(8,128)(2,1)S(1)}, bf16[480,768]{1,0:T(8,128)(2,1)S(1)}, u32[]{:S(2)}, u32[]{:S(2)}) collective-permute-start(bf16[480,768]{1,0:T(8,128)(2,1)S(1)} %get-tuple-element.25), channel_id=1, source_target_pairs={{0,1},{1,0},{2,3},{3,2},{4,5},{5,4},{6,7},{7,6},{8,9},{9,8},{10,11... | collective-permute-start | bytes 2211848 | tf_op jit(solution)/shard_map/ppermute | solution.py:89
  63.0 1.9 %collective-permute-start.19 = (bf16[288,768]{1,0:T(8,128)(2,1)S(1)}, bf16[288,768]{1,0:T(8,128)(2,1)S(1)}, u32[]{:S(2)}, u32[]{:S(2)}) collective-permute-start(bf16[288,768]{1,0:T(8,128)(2,1)S(1)} %get-tuple-element.29), channel_id=1, source_target_pairs={{0,1},{1,0},{2,3},{3,2},{4,5},{5,4},{6,7},{7,6},{8,9},{9,8},{10,11... | collective-permute-start | bytes 1327112 | tf_op jit(solution)/shard_map/ppermute | solution.py:89
  63.2 4.0 %collective-permute-start.27 = (bf16[288,768]{1,0:T(8,128)(2,1)S(1)}, bf16[288,768]{1,0:T(8,128)(2,1)S(1)}, u32[]{:S(2)}, u32[]{:S(2)}) collective-permute-start(bf16[288,768]{1,0:T(8,128)(2,1)S(1)} %get-tuple-element.33), channel_id=1, source_target_pairs={{0,1},{1,0},{2,3},{3,2},{4,5},{5,4},{6,7},{7,6},{8,9},{9,8},{10,11... | collective-permute-start | bytes 1327112 | tf_op jit(solution)/shard_map/ppermute | solution.py:89
  63.6 16.9 %collective-permute-start.21 = (bf16[240,768]{1,0:T(8,128)(2,1)S(1)}, bf16[240,768]{1,0:T(8,128)(2,1)S(1)}, u32[]{:S(2)}, u32[]{:S(2)}) collective-permute-start(bf16[240,768]{1,0:T(8,128)(2,1)S(1)} %shard_map.150.refs_10_), channel_id=1, source_target_pairs={{0,2},{1,7},{2,4},{3,1},{4,6},{5,3},{6,0},{7,5},{8,10},{9,15},{10,... | collective-permute-start | bytes 1105928 | tf_op jit(solution)/shard_map/ppermute | solution.py:85
  64.9 19.4 %collective-permute-start.28 = (bf16[144,768]{1,0:T(8,128)(2,1)S(1)}, bf16[144,768]{1,0:T(8,128)(2,1)S(1)}, u32[]{:S(2)}, u32[]{:S(2)}) collective-permute-start(bf16[144,768]{1,0:T(8,128)(2,1)S(1)} %shard_map.156.refs_1_), channel_id=1, source_target_pairs={{0,6},{1,3},{2,0},{3,5},{4,2},{5,7},{6,4},{7,1},{8,14},{9,11},{10,... | collective-permute-start | bytes 663560 | tf_op jit(solution)/shard_map/ppermute | solution.py:85
  67.0 17.3 %collective-permute-start.30 = (bf16[144,768]{1,0:T(8,128)(2,1)S(1)}, bf16[144,768]{1,0:T(8,128)(2,1)S(1)}, u32[]{:S(2)}, u32[]{:S(2)}) collective-permute-start(bf16[144,768]{1,0:T(8,128)(2,1)S(1)} %shard_map.158), channel_id=1, source_target_pairs={{0,4},{1,5},{2,6},{3,7},{4,0},{5,1},{6,2},{7,3},{8,12},{9,13},{10,... | collective-permute-start | bytes 663560 | tf_op jit(solution)/shard_map/ppermute | solution.py:85
  67.2 18.0 %collective-permute-start.29 = (bf16[144,768]{1,0:T(8,128)(2,1)S(1)}, bf16[144,768]{1,0:T(8,128)(2,1)S(1)}, u32[]{:S(2)}, u32[]{:S(2)}) collective-permute-start(bf16[144,768]{1,0:T(8,128)(2,1)S(1)} %shard_map.157), channel_id=1, source_target_pairs={{0,2},{1,7},{2,4},{3,1},{4,6},{5,3},{6,0},{7,5},{8,10},{9,15},{10,... | collective-permute-start | bytes 663560 | tf_op jit(solution)/shard_map/ppermute | solution.py:85
  80.6 10.1 %collective-permute-start.22 = (bf16[240,768]{1,0:T(8,128)(2,1)S(1)}, bf16[240,768]{1,0:T(8,128)(2,1)S(1)}, u32[]{:S(2)}, u32[]{:S(2)}) collective-permute-start(bf16[240,768]{1,0:T(8,128)(2,1)S(1)} %shard_map.154), channel_id=1, source_target_pairs={{0,2},{1,7},{2,4},{3,1},{4,6},{5,3},{6,0},{7,5},{8,10},{9,15},{10,... | collective-permute-start | bytes 1105928 | tf_op jit(solution)/shard_map/ppermute | solution.py:85
  80.8 9.9 %collective-permute-start.20 = (bf16[240,768]{1,0:T(8,128)(2,1)S(1)}, bf16[240,768]{1,0:T(8,128)(2,1)S(1)}, u32[]{:S(2)}, u32[]{:S(2)}) collective-permute-start(bf16[240,768]{1,0:T(8,128)(2,1)S(1)} %shard_map.152), channel_id=1, source_target_pairs={{0,6},{1,3},{2,0},{3,5},{4,2},{5,7},{6,4},{7,1},{8,14},{9,11},{10,... | collective-permute-start | bytes 1105928 | tf_op jit(solution)/shard_map/ppermute | solution.py:85
  85.4 10.6 %collective-permute-start.31 = (bf16[48,768]{1,0:T(8,128)(2,1)S(1)}, bf16[48,768]{1,0:T(8,128)(2,1)S(1)}, u32[]{:S(2)}, u32[]{:S(2)}) collective-permute-start(bf16[48,768]{1,0:T(8,128)(2,1)S(1)} %get-tuple-element.44), channel_id=1, source_target_pairs={{0,160},{8,168},{16,176},{24,184},{32,192},{40,200},{48,208},{56,2... | collective-permute-start | bytes 221192 | tf_op jit(solution)/shard_map/ppermute | solution.py:77
  85.8 11.2 %collective-permute-start.33 = (bf16[48,768]{1,0:T(8,128)(2,1)S(1)}, bf16[48,768]{1,0:T(8,128)(2,1)S(1)}, u32[]{:S(2)}, u32[]{:S(2)}) collective-permute-start(bf16[48,768]{1,0:T(8,128)(2,1)S(1)} %get-tuple-element.45), channel_id=1, source_target_pairs={{0,96},{8,104},{16,112},{24,120},{32,128},{40,136},{48,144},{56,15... | collective-permute-start | bytes 221192 | tf_op jit(solution)/shard_map/ppermute | solution.py:77
  89.3 10.0 %collective-permute-start.32 = (bf16[48,768]{1,0:T(8,128)(2,1)S(1)}, bf16[48,768]{1,0:T(8,128)(2,1)S(1)}, u32[]{:S(2)}, u32[]{:S(2)}) collective-permute-start(bf16[48,768]{1,0:T(8,128)(2,1)S(1)} %get-tuple-element.46), channel_id=1, source_target_pairs={{0,128},{8,136},{16,144},{24,152},{32,160},{40,168},{48,176},{56,1... | collective-permute-start | bytes 221192 | tf_op jit(solution)/shard_map/ppermute | solution.py:77
  91.0 8.3 %collective-permute-start.24 = (bf16[48,768]{1,0:T(8,128)(2,1)S(1)}, bf16[48,768]{1,0:T(8,128)(2,1)S(1)}, u32[]{:S(2)}, u32[]{:S(2)}) collective-permute-start(bf16[48,768]{1,0:T(8,128)(2,1)S(1)} %get-tuple-element.41), channel_id=1, source_target_pairs={{0,32},{8,40},{16,48},{24,56},{32,64},{40,72},{48,80},{56,88},{64,... | collective-permute-start | bytes 221192 | tf_op jit(solution)/shard_map/ppermute | solution.py:77
  92.6 8.2 %collective-permute-start.26 = (bf16[48,768]{1,0:T(8,128)(2,1)S(1)}, bf16[48,768]{1,0:T(8,128)(2,1)S(1)}, u32[]{:S(2)}, u32[]{:S(2)}) collective-permute-start(bf16[48,768]{1,0:T(8,128)(2,1)S(1)} %get-tuple-element.42), channel_id=1, source_target_pairs={{0,64},{8,72},{16,80},{24,88},{32,96},{40,104},{48,112},{56,120},{... | collective-permute-start | bytes 221192 | tf_op jit(solution)/shard_map/ppermute | solution.py:77
  95.9 6.1 %collective-permute-start.25 = (bf16[48,768]{1,0:T(8,128)(2,1)S(1)}, bf16[48,768]{1,0:T(8,128)(2,1)S(1)}, u32[]{:S(2)}, u32[]{:S(2)}) collective-permute-start(bf16[48,768]{1,0:T(8,128)(2,1)S(1)} %get-tuple-element.43), channel_id=1, source_target_pairs={{0,192},{8,200},{16,208},{24,216},{32,224},{40,232},{48,240},{56,2... | collective-permute-start | bytes 221192 | tf_op jit(solution)/shard_map/ppermute | solution.py:77
  97.0 6.7 %collective-permute-start.23 = (bf16[48,768]{1,0:T(8,128)(2,1)S(1)}, bf16[48,768]{1,0:T(8,128)(2,1)S(1)}, u32[]{:S(2)}, u32[]{:S(2)}) collective-permute-start(bf16[48,768]{1,0:T(8,128)(2,1)S(1)} %shard_map.155), channel_id=1, source_target_pairs={{0,224},{8,232},{16,240},{24,248},{32,0},{40,8},{48,16},{56,24},{6... | collective-permute-start | bytes 221192 | tf_op jit(solution)/shard_map/ppermute | solution.py:77
  103.8 5.8 %collective-permute-start.34 = (bf16[12,768]{1,0:T(8,128)(2,1)S(1)}, bf16[12,768]{1,0:T(8,128)(2,1)S(1)}, u32[]{:S(2)}, u32[]{:S(2)}) collective-permute-start(bf16[12,768]{1,0:T(8,128)(2,1)S(1)} %get-tuple-element.47), channel_id=1, source_target_pairs={{0,24},{8,0},{16,8},{24,16},{32,56},{40,32},{48,40},{56,48},{64,88... | collective-permute-start | bytes 55304 | tf_op jit(solution)/shard_map/ppermute | solution.py:70
  105.8 3.8 %collective-permute-start.36 = (bf16[12,768]{1,0:T(8,128)(2,1)S(1)}, bf16[12,768]{1,0:T(8,128)(2,1)S(1)}, u32[]{:S(2)}, u32[]{:S(2)}) collective-permute-start(bf16[12,768]{1,0:T(8,128)(2,1)S(1)} %get-tuple-element.48), channel_id=1, source_target_pairs={{0,8},{8,16},{16,24},{24,0},{32,40},{40,48},{48,56},{56,32},{64,72... | collective-permute-start | bytes 55304 | tf_op jit(solution)/shard_map/ppermute | solution.py:70
  105.9 5.5 %collective-permute-start.35 = (bf16[12,768]{1,0:T(8,128)(2,1)S(1)}, bf16[12,768]{1,0:T(8,128)(2,1)S(1)}, u32[]{:S(2)}, u32[]{:S(2)}) collective-permute-start(bf16[12,768]{1,0:T(8,128)(2,1)S(1)} %get-tuple-element.49), channel_id=1, source_target_pairs={{0,16},{8,24},{16,0},{24,8},{32,48},{40,56},{48,32},{56,40},{64,80... | collective-permute-start | bytes 55304 | tf_op jit(solution)/shard_map/ppermute | solution.py:70
